TPU v7x, 128 devices: a whole 4x4x4 slice. The times are simulated.
128 devices in a mesh: dp: 8 (over z_lo, x), ctx: 16 (over z_hi, y, core).
Axes of the slice: x: 4, y: 4, z: 4 (z_hi: 2, z_lo: 2; z = z_hi * 2 + z_lo), core: 2. Of those that a mesh axis runs over, the one named last changes fastest.
Arguments:
- hidden_in: bfloat16 [16384, 576], P(('dp', 'ctx')), may hold values from -6 to 6
- positions: int32 [16384], P('dp'), may hold values from 0 to 2047, as said below
- attn_gain: bfloat16 [2, 576], P(None, 'dp'), may hold values from 0.25 to 1.75
- w_query: bfloat16 [2, 576, 576], P(None, 'dp'), may hold values from -0.25 to 0.25
- w_key: bfloat16 [2, 576, 192], P(None, 'dp'), may hold values from -0.25 to 0.25
- w_value: bfloat16 [2, 576, 192], P(None, 'dp'), may hold values from -0.25 to 0.25
- w_output: bfloat16 [2, 576, 576], P(None, 'dp'), may hold values from -4 to 4
- ffn_gain: bfloat16 [2, 576], P(None, 'dp'), may hold values from 0.25 to 1.75
- w_gate: bfloat16 [2, 576, 1536], P(None, 'dp'), may hold values from -0.25 to 0.25
- w_up: bfloat16 [2, 576, 1536], P(None, 'dp'), may hold values from -0.25 to 0.25
- w_down: bfloat16 [2, 1536, 576], P(None, 'dp'), may hold values from -0.15625 to 0.15625
- grad_out: bfloat16 [16384, 576], P(('dp', 'ctx')), may hold values from -6 to 6
Outputs:
- hidden_out: bfloat16 [16384, 576], P(('dp', 'ctx'))
- grad_hidden: float32 [16384, 576], P(('dp', 'ctx'))
- grad_attn_gain: float32 [2, 576], P(None, 'dp')
- grad_query: float32 [2, 576, 576], P(None, 'dp')
- grad_key: float32 [2, 576, 192], P(None, 'dp')
- grad_value: float32 [2, 576, 192], P(None, 'dp')
- grad_output: float32 [2, 576, 576], P(None, 'dp')
- grad_ffn_gain: float32 [2, 576], P(None, 'dp')
- grad_gate: float32 [2, 576, 1536], P(None, 'dp')
- grad_up: float32 [2, 576, 1536], P(None, 'dp')
- grad_down: float32 [2, 1536, 576], P(None, 'dp')
Inputs may be any that keep to these rules, and one draw needn't show every extreme that they name: Rows s*2048 to (s+1)*2048 - 1 form sequence s and hold each of its positions once. Its positions are cut into 32 blocks of 64 consecutive positions; each aligned run of 128 rows holds, in increasing order, block j followed by block 31-j, with a different j in each run of a sequence.
All inputs are finite; a program needn't handle non-finite values.
Results may differ from a plain program's by a relative error of at most 0.028.
Values may be sent and summed in bfloat16 or wider, within the bound.
A program may use at most 192 MiB of HBM per device.

v0:
```python
import jax
import jax.numpy as jnp
from jax import lax
from jax.sharding import PartitionSpec as P

D = 576
HEADS = 9
KV_HEADS = 3
HEAD_DIM = 64
LAYERS = 2


eps_norm = 1e-05
rope_base = 100000.0


def as_sent(x):
    return jax.tree.map(lambda a: a.astype(jnp.bfloat16) if a.dtype == jnp.float32 else a, x)


def normed(values, gain):
    factor = lax.rsqrt(jnp.mean(values * values, axis=-1, keepdims=True) + eps_norm)
    return values * factor * gain


def angles(place, head_dim):
    half = head_dim // 2
    freq = jnp.exp(-jnp.log(rope_base) * (2.0 * jnp.arange(half, dtype=jnp.float32) / head_dim))
    angle = place.astype(jnp.float32)[:, None] * freq[None, :]
    return (jnp.cos(angle)[:, None, :], jnp.sin(angle)[:, None, :])


def rotate(values, cosine, sine):
    half = values.shape[-1] // 2
    first = values[..., :half]
    second = values[..., half:]
    return jnp.concatenate(
        [first * cosine - second * sine, second * cosine + first * sine], axis=-1
    )


def swiglu(gate, upper):
    return jax.nn.silu(gate) * upper


def dot_plain(left, right):
    return jnp.dot(left, right, preferred_element_type=jnp.float32)


def dot_left(left, right):
    return lax.dot_general(
        left, right, (((0,), (0,)), ((), ())), preferred_element_type=jnp.float32
    )


def dot_right(left, right):
    return lax.dot_general(
        left, right, (((1,), (1,)), ((), ())), preferred_element_type=jnp.float32
    )


def group_scores(query_group, key_group, allowed):
    scores = jnp.einsum(
        "tjd,sd->jts", query_group, key_group, preferred_element_type=jnp.float32
    ) * HEAD_DIM ** (-0.5)
    return jnp.where(allowed[None], scores, -1000000000.0)


def forward_layer(hidden, weights, cosine, sine, allowed):
    gain_attn, query_w, key_w, value_w, output_w, gain_ffn, gate_w, up_w, down_w = weights
    rows = hidden.shape[0]
    group = HEADS // KV_HEADS
    normal_a = normed(hidden, gain_attn.astype(jnp.float32)).astype(jnp.bfloat16)
    query = dot_plain(normal_a, query_w).reshape(rows, HEADS, HEAD_DIM)
    keys = dot_plain(normal_a, key_w).reshape(rows, KV_HEADS, HEAD_DIM)
    values = dot_plain(normal_a, value_w).astype(jnp.bfloat16)
    query = rotate(query, cosine, sine).astype(jnp.bfloat16)
    keys = rotate(keys, cosine, sine).astype(jnp.bfloat16).reshape(rows, KV_HEADS * HEAD_DIM)
    keys_all, values_all = (
        lax.all_gather(keys, "ctx", axis=0, tiled=True),
        lax.all_gather(values, "ctx", axis=0, tiled=True),
    )
    outputs = []
    totals = []
    for head in range(KV_HEADS):
        query_group = query[:, head * group : (head + 1) * group, :]
        key_group = keys_all[:, head * HEAD_DIM : (head + 1) * HEAD_DIM]
        value_group = values_all[:, head * HEAD_DIM : (head + 1) * HEAD_DIM]
        scores = group_scores(query_group, key_group, allowed)
        top = jnp.max(scores, axis=-1, keepdims=True)
        expo = jnp.exp(scores - top)
        total = jnp.sum(expo, axis=-1, keepdims=True)
        probs = (expo / total).astype(jnp.bfloat16)
        totals.append(top + jnp.log(total))
        outputs.append(
            jnp.einsum("jts,sd->tjd", probs, value_group, preferred_element_type=jnp.float32)
        )
    mixed = jnp.concatenate(outputs, axis=1).reshape(rows, D).astype(jnp.bfloat16)
    middle_h = hidden + dot_plain(mixed, output_w)
    normal_b = normed(middle_h, gain_ffn.astype(jnp.float32)).astype(jnp.bfloat16)
    gate = dot_plain(normal_b, gate_w)
    upper = dot_plain(normal_b, up_w)
    middle = swiglu(gate, upper).astype(jnp.bfloat16)
    result = middle_h + dot_plain(middle, down_w)
    kept = (
        hidden,
        normal_a,
        query,
        keys_all,
        values_all,
        totals,
        mixed,
        middle_h,
        normal_b,
        gate,
        upper,
        middle,
    )
    return (kept, result)


def backward_layer(grad, kept, weights, cosine, sine, allowed):
    gain_attn, query_w, key_w, value_w, output_w, gain_ffn, gate_w, up_w, down_w = weights
    (
        hidden,
        normal_a,
        query,
        keys_all,
        values_all,
        totals,
        mixed,
        middle_h,
        normal_b,
        gate,
        upper,
        middle,
    ) = kept
    rows = hidden.shape[0]
    group = HEADS // KV_HEADS
    grad_z = grad.astype(jnp.bfloat16)
    grad_down_w = dot_left(middle, grad_z)
    grad_middle = dot_right(grad_z, down_w)
    unused, swiglu_pull = jax.vjp(swiglu, gate, upper)
    grad_gate, grad_upper = swiglu_pull(grad_middle)
    grad_gate = grad_gate.astype(jnp.bfloat16)
    grad_upper = grad_upper.astype(jnp.bfloat16)
    grad_gate_w = dot_left(normal_b, grad_gate)
    grad_up_w = dot_left(normal_b, grad_upper)
    grad_normal_b = dot_right(grad_gate, gate_w) + dot_right(grad_upper, up_w)
    unused, norm_pull = jax.vjp(normed, middle_h, gain_ffn.astype(jnp.float32))
    grad_middle_h, grad_gain_ffn = norm_pull(grad_normal_b)
    grad_middle_h = grad + grad_middle_h
    grad_y = grad_middle_h.astype(jnp.bfloat16)
    grad_output_w = dot_left(mixed, grad_y)
    grad_mixed = dot_right(grad_y, output_w).astype(jnp.bfloat16).reshape(rows, HEADS, HEAD_DIM)
    query_parts = []
    key_parts = []
    value_parts = []
    for head in range(KV_HEADS):
        query_group = query[:, head * group : (head + 1) * group, :]
        key_group = keys_all[:, head * HEAD_DIM : (head + 1) * HEAD_DIM]
        value_group = values_all[:, head * HEAD_DIM : (head + 1) * HEAD_DIM]
        grad_group = grad_mixed[:, head * group : (head + 1) * group, :]
        scores = group_scores(query_group, key_group, allowed)
        probs = jnp.exp(scores - totals[head])
        grad_probs = jnp.einsum(
            "tjd,sd->jts", grad_group, value_group, preferred_element_type=jnp.float32
        )
        inner = jnp.sum(probs * grad_probs, axis=-1, keepdims=True)
        grad_scores = (probs * (grad_probs - inner) * HEAD_DIM ** (-0.5)).astype(jnp.bfloat16)
        value_parts.append(
            jnp.einsum(
                "jts,tjd->sd",
                probs.astype(jnp.bfloat16),
                grad_group,
                preferred_element_type=jnp.float32,
            )
        )
        query_parts.append(
            jnp.einsum("jts,sd->tjd", grad_scores, key_group, preferred_element_type=jnp.float32)
        )
        key_parts.append(
            jnp.einsum("jts,tjd->sd", grad_scores, query_group, preferred_element_type=jnp.float32)
        )
    grad_keys_all = jnp.concatenate(key_parts, axis=1)
    grad_values_all = jnp.concatenate(value_parts, axis=1)
    grad_keys, grad_values = (
        lax.psum_scatter(
            grad_keys_all.astype(jnp.bfloat16), "ctx", scatter_dimension=0, tiled=True
        ).astype(jnp.float32),
        lax.psum_scatter(
            grad_values_all.astype(jnp.bfloat16), "ctx", scatter_dimension=0, tiled=True
        ).astype(jnp.float32),
    )
    grad_query = jnp.concatenate(query_parts, axis=1)
    grad_query = rotate(grad_query, cosine, -sine).reshape(rows, D).astype(jnp.bfloat16)
    grad_keys = (
        rotate(grad_keys.reshape(rows, KV_HEADS, HEAD_DIM), cosine, -sine)
        .reshape(rows, KV_HEADS * HEAD_DIM)
        .astype(jnp.bfloat16)
    )
    grad_values = grad_values.astype(jnp.bfloat16)
    grad_query_w = dot_left(normal_a, grad_query)
    grad_key_w = dot_left(normal_a, grad_keys)
    grad_value_w = dot_left(normal_a, grad_values)
    grad_normal_a = (
        dot_right(grad_query, query_w)
        + dot_right(grad_keys, key_w)
        + dot_right(grad_values, value_w)
    )
    unused, norm_pull = jax.vjp(normed, hidden, gain_attn.astype(jnp.float32))
    grad_hidden, grad_gain_attn = norm_pull(grad_normal_a)
    parts = (
        grad_gain_attn,
        grad_query_w,
        grad_key_w,
        grad_value_w,
        grad_output_w,
        grad_gain_ffn,
        grad_gate_w,
        grad_up_w,
        grad_down_w,
    )
    return (grad_middle_h + grad_hidden, parts)


def reduce_grads(parts, data_count, context_count):
    flat = jnp.concatenate([item.reshape(data_count, -1) for item in parts], axis=1)
    width = flat.shape[1]
    padding = -width % context_count
    share = (width + padding) // context_count
    piece = lax.psum_scatter(
        flat.reshape(data_count, context_count, share).astype(jnp.bfloat16),
        "ctx",
        scatter_dimension=1,
        tiled=True,
    ).astype(jnp.float32)
    piece = lax.psum_scatter(
        piece.reshape(data_count, share).astype(jnp.bfloat16), "dp", scatter_dimension=0, tiled=True
    ).astype(jnp.float32)
    summed = (
        lax.all_gather(piece.astype(jnp.bfloat16), "ctx", axis=0, tiled=True)
        .astype(piece.dtype)
        .reshape(-1)
    )
    results = []
    offset = 0
    for item in parts:
        length = item.size // data_count
        shape = (item.shape[0] // data_count,) + item.shape[1:]
        results.append(summed[offset : offset + length].reshape(shape))
        offset = offset + length
    return results


def body(
    hidden_in,
    positions,
    attn_gain,
    w_query,
    w_key,
    w_value,
    w_output,
    ffn_gain,
    w_gate,
    w_up,
    w_down,
    grad_out,
):
    data_count = lax.axis_size("dp")
    context_count = lax.axis_size("ctx")
    rows = hidden_in.shape[0]
    own_place = lax.dynamic_slice_in_dim(positions, lax.axis_index("ctx") * rows, rows)
    cosine, sine = angles(own_place, HEAD_DIM)
    allowed = own_place[:, None] >= positions[None, :]
    shards = (attn_gain, w_query, w_key, w_value, w_output, ffn_gain, w_gate, w_up, w_down)
    hidden = hidden_in.astype(jnp.float32)
    stored = []
    gathered_all = []
    for index in range(LAYERS):
        pieces = tuple((item[index] for item in shards))
        weights = jax.tree.map(
            lambda part, own: part.astype(own.dtype),
            lax.all_gather(as_sent(pieces), "dp", axis=0, tiled=True),
            pieces,
        )
        kept, hidden = forward_layer(hidden, weights, cosine, sine, allowed)
        stored.append(kept)
        gathered_all.append(weights)
    hidden_out = hidden.astype(jnp.bfloat16)
    grad = grad_out.astype(jnp.float32)
    reduced = [None] * LAYERS
    for index in reversed(range(LAYERS)):
        pieces = tuple((item[index] for item in shards))
        weights = jax.tree.map(
            lambda part, own: part.astype(own.dtype),
            lax.all_gather(as_sent(pieces), "dp", axis=0, tiled=True),
            pieces,
        )
        grad, parts = backward_layer(grad, stored[index], weights, cosine, sine, allowed)
        reduced[index] = reduce_grads(parts, data_count, context_count)
    stacked = [
        jnp.stack([reduced[index][slot] for index in range(LAYERS)], axis=0) for slot in range(9)
    ]
    return (
        hidden_out,
        grad,
        stacked[0],
        stacked[1],
        stacked[2],
        stacked[3],
        stacked[4],
        stacked[5],
        stacked[6],
        stacked[7],
        stacked[8],
    )


def solution(mesh):
    placed = (
        P(("dp", "ctx"), None),
        P("dp"),
        P(None, "dp"),
        P(None, "dp", None),
        P(None, "dp", None),
        P(None, "dp", None),
        P(None, "dp", None),
        P(None, "dp"),
        P(None, "dp", None),
        P(None, "dp", None),
        P(None, "dp", None),
        P(("dp", "ctx"), None),
    )
    return jax.shard_map(
        body,
        mesh=mesh,
        in_specs=placed,
        out_specs=(
            P(("dp", "ctx"), None),
            P(("dp", "ctx"), None),
            P(None, "dp"),
            P(None, "dp", None),
            P(None, "dp", None),
            P(None, "dp", None),
            P(None, "dp", None),
            P(None, "dp"),
            P(None, "dp", None),
            P(None, "dp", None),
            P(None, "dp", None),
        ),
        check_vma=False,
    )
```

profile of v0, /device:TPU:1, one launch (start us, length us, event | category | flops | bytes accessed | tf_op | source)
XLA Modules:
  0.0 1206.6 jit_solution(18416811507223020755)
XLA Ops:
  17.3 18.8 %all-reduce.8 = (bf16[576]{0:T(1024)(128)(2,1)S(1)}, bf16[576]{0:T(1024)(128)(2,1)}, bf16[576]{0:T(1024)(128)(2,1)}, bf16[576]{0:T(1024)(128)(2,1)}) all-reduce(bf16[576]{0:T(1024)(128)(2,1)S(1)} %dynamic-update-slice, bf16[576]{0:T(1024)(128)(2,1)S(1)} %dynamic-update-slice.1, ...), channel_id=2, replica_groups=mesh['dp'=8,'ctx'=16] {'dp'}, use_global_device_ids=true, to_apply=%add | all-reduce | flops 2304 | bytes 9216
  37.8 23.8 %all-gather.2 = bf16[1,576,192]{2,1,0:T(8,128)(2,1)S(1)} all-gather(bf16[1,72,192]{2,1,0:T(8,128)(2,1)S(1)} %get-tuple-element.79), channel_id=4, replica_groups=mesh['dp'=8,'ctx'=16] {'dp'}, dimensions={1}, use_global_device_ids=true | all-gather | bytes 248832 | tf_op jit(solution)/shard_map/all_gather | solution.py:284
  62.2 36.6 %all_gather.94 = bf16[2048,192]{0,1:T(8,128)(2,1)S(1)} all-gather(bf16[128,192]{0,1:T(8,128)(2,1)S(1)} %bitcast.557), channel_id=1, replica_groups=mesh['dp'=8,'ctx'=16] {'ctx'}, dimensions={0}, use_global_device_ids=true | all-gather | bytes 835584 | tf_op jit(solution)/shard_map/all_gather | solution.py:80
  98.8 25.6 %all-gather.3 = bf16[1,576,576]{2,1,0:T(8,128)(2,1)S(1)} all-gather(bf16[1,72,576]{2,1,0:T(8,128)(2,1)S(1)} %get-tuple-element.67), channel_id=5, replica_groups=mesh['dp'=8,'ctx'=16] {'dp'}, dimensions={1}, use_global_device_ids=true | all-gather | bytes 746496 | tf_op jit(solution)/shard_map/all_gather | solution.py:284
  127.6 23.3 %all-gather.1 = bf16[1,576,192]{2,1,0:T(8,128)(2,1)S(1)} all-gather(bf16[1,72,192]{2,1,0:T(8,128)(2,1)S(1)} %get-tuple-element.77), channel_id=3, replica_groups=mesh['dp'=8,'ctx'=16] {'dp'}, dimensions={1}, use_global_device_ids=true | all-gather | bytes 248832 | tf_op jit(solution)/shard_map/all_gather | solution.py:284
  152.0 34.5 %all_gather.92 = bf16[2048,192]{0,1:T(8,128)(2,1)S(1)} all-gather(bf16[128,192]{0,1:T(8,128)(2,1)S(1)} %convolution_convert_fusion.17), channel_id=1, replica_groups=mesh['dp'=8,'ctx'=16] {'ctx'}, dimensions={0}, use_global_device_ids=true | all-gather | bytes 835584 | tf_op jit(solution)/shard_map/all_gather | solution.py:81
  194.7 26.0 %all-gather.10 = bf16[1,576,192]{2,1,0:T(8,128)(2,1)} all-gather(bf16[1,72,192]{2,1,0:T(8,128)(2,1)} %get-tuple-element.76), channel_id=12, replica_groups=mesh['dp'=8,'ctx'=16] {'dp'}, dimensions={1}, use_global_device_ids=true | all-gather | bytes 248832 | tf_op jit(solution)/shard_map/all_gather | solution.py:284
  220.6 24.9 %all-gather.11 = bf16[1,576,192]{2,1,0:T(8,128)(2,1)} all-gather(bf16[1,72,192]{2,1,0:T(8,128)(2,1)S(1)} %copy-done.72), channel_id=13, replica_groups=mesh['dp'=8,'ctx'=16] {'dp'}, dimensions={1}, use_global_device_ids=true | all-gather | bytes 248832 | tf_op jit(solution)/shard_map/all_gather | solution.py:284
  245.6 27.8 %all-gather.13 = bf16[1,576,576]{2,1,0:T(8,128)(2,1)} all-gather(bf16[1,72,576]{2,1,0:T(8,128)(2,1)S(1)} %get-tuple-element.64), channel_id=15, replica_groups=mesh['dp'=8,'ctx'=16] {'dp'}, dimensions={1}, use_global_device_ids=true | all-gather | bytes 746496 | tf_op jit(solution)/shard_map/all_gather | solution.py:284
  273.4 25.7 %all-gather.12 = bf16[1,576,576]{2,1,0:T(8,128)(2,1)} all-gather(bf16[1,72,576]{2,1,0:T(8,128)(2,1)S(1)} %copy-done.66), channel_id=14, replica_groups=mesh['dp'=8,'ctx'=16] {'dp'}, dimensions={1}, use_global_device_ids=true | all-gather | bytes 746496 | tf_op jit(solution)/shard_map/all_gather | solution.py:284
  299.0 23.9 %all-gather.4 = bf16[1,576,576]{2,1,0:T(8,128)(2,1)S(1)} all-gather(bf16[1,72,576]{2,1,0:T(8,128)(2,1)S(1)} %get-tuple-element.65), channel_id=6, replica_groups=mesh['dp'=8,'ctx'=16] {'dp'}, dimensions={1}, use_global_device_ids=true | all-gather | bytes 746496 | tf_op jit(solution)/shard_map/all_gather | solution.py:284
  335.0 47.9 %all_gather.105 = bf16[2048,192]{0,1:T(8,128)(2,1)S(1)} all-gather(bf16[128,192]{0,1:T(8,128)(2,1)S(1)} %bitcast.558), channel_id=1, replica_groups=mesh['dp'=8,'ctx'=16] {'ctx'}, dimensions={0}, use_global_device_ids=true | all-gather | bytes 835584 | tf_op jit(solution)/shard_map/all_gather | solution.py:80
  385.4 22.7 %all_gather.103 = bf16[2048,192]{0,1:T(8,128)(2,1)S(1)} all-gather(bf16[128,192]{0,1:T(8,128)(2,1)S(1)} %convolution_convert_fusion.16), channel_id=1, replica_groups=mesh['dp'=8,'ctx'=16] {'ctx'}, dimensions={0}, use_global_device_ids=true | all-gather | bytes 835584 | tf_op jit(solution)/shard_map/all_gather | solution.py:81
  439.9 10.7 copy.137
  521.1 14.2 %reduce-scatter.19.cloned.1.call-done = bf16[128,192]{1,0:T(8,128)(2,1)} async-done(((bf16[2048,192]{1,0:T(8,128)(2,1)}), bf16[128,192]{1,0:T(8,128)(2,1)}) %reduce-scatter.19.cloned.1.call-update) | async-done | bytes 49168
  538.3 67.1 %reduce-scatter.21.cloned.1.call-done = bf16[128,192]{1,0:T(8,128)(2,1)} async-done(((bf16[2048,192]{1,0:T(8,128)(2,1)}), bf16[128,192]{1,0:T(8,128)(2,1)}) %reduce-scatter.21.cloned.1.call-update) | async-done | bytes 49168
  728.3 15.1 %reshape.553 = bf16[3540096]{0:T(1024)(128)(2,1)} reshape(bf16[8,442512]{1,0:T(8,128)(2,1)} %dynamic-update-slice.12) | data formatting | bytes 14160384
  743.4 17.4 %convert_element_type.257 = bf16[8,16,27657]{2,1,0:T(8,128)(2,1)} reshape(bf16[3540096]{0:T(1024)(128)(2,1)} %reshape.553) | data formatting | bytes 14160384 | tf_op jit(solution)/shard_map/convert_element_type | solution.py:233
  877.2 15.1 %reshape.557 = bf16[3540096]{0:T(1024)(128)(2,1)} reshape(bf16[8,442512]{1,0:T(8,128)(2,1)} %dynamic-update-slice.21) | data formatting | bytes 14160384
  892.4 17.0 %convert_element_type.255 = bf16[8,16,27657]{2,1,0:T(8,128)(2,1)} reshape(bf16[3540096]{0:T(1024)(128)(2,1)} %reshape.557) | data formatting | bytes 14160384 | tf_op jit(solution)/shard_map/convert_element_type | solution.py:233
  916.6 109.6 %reduce-scatter.27.cloned.1.call-done = bf16[8,1,27657]{2,0,1:T(8,128)(2,1)} async-done(((bf16[8,16,27657]{2,0,1:T(8,128)(2,1)}), bf16[8,1,27657]{2,0,1:T(8,128)(2,1)}) %reduce-scatter.27.cloned.1.call-update) | async-done | bytes 442528
  1029.6 70.8 %all-reduce.12.cloned.1.call-done = (bf16[8,27657]{1,0:T(8,128)(2,1)}, bf16[8,27657]{1,0:T(8,128)(2,1)}) async-done(((bf16[8,27657]{1,0:T(8,128)(2,1)}, bf16[8,27657]{1,0:T(8,128)(2,1)}), (bf16[8,27657]{1,0:T(8,128)(2,1)}, bf16[8,27657]{1,0:T(8,128)(2,1)})) %all-reduce.12.cloned.1.call-update) | async-done | bytes 885040
  1102.2 34.6 %all-gather.18 = bf16[16,1,27657]{2,1,0:T(2,128)(2,1)S(1)} all-gather(bf16[1,1,27657]{2,1,0:T(2,128)(2,1)S(1)} %dynamic-slice_bitcast_fusion.1), channel_id=1, replica_groups=mesh['dp'=8,'ctx'=16] {'ctx'}, dimensions={0}, use_global_device_ids=true | all-gather | bytes 940338 | tf_op jit(solution)/shard_map/all_gather | solution.py:242
  1148.1 25.2 %all-gather.19 = bf16[16,1,27657]{2,1,0:T(2,128)(2,1)S(1)} all-gather(bf16[1,1,27657]{2,1,0:T(2,128)(2,1)S(1)} %dynamic-slice_bitcast_fusion), channel_id=1, replica_groups=mesh['dp'=8,'ctx'=16] {'ctx'}, dimensions={0}, use_global_device_ids=true | all-gather | bytes 940338 | tf_op jit(solution)/shard_map/all_gather | solution.py:242
  (475 shorter events, 431.8 us)
Async XLA Ops:
  7.3 317.9 %all-gather.27.cloned.1.call-start = ((), (), s32[]{:S(2)}) async-start(), calls=%async_computation.6 | async-start | bytes 1990656 | tf_op jit(solution)/shard_map/all_gather | solution.py:284
  9.3 318.8 %all-gather.29.cloned.1.call-start = ((), (), s32[]{:S(2)}) async-start(), calls=%async_computation.7 | async-start | bytes 1990656 | tf_op jit(solution)/shard_map/all_gather | solution.py:284
  11.2 320.1 %all-gather.31.cloned.1.call-start = ((), (), s32[]{:S(2)}) async-start(), calls=%async_computation.8 | async-start | bytes 2211840 | tf_op jit(solution)/shard_map/all_gather | solution.py:284
  13.2 400.7 %all-gather.35.cloned.1.call-start = ((), (), s32[]{:S(2)}) async-start(), calls=%async_computation.10 | async-start | bytes 1990656 | tf_op jit(solution)/shard_map/all_gather | solution.py:284
  13.7 403.1 %all-gather.37.cloned.1.call-start = ((), (), s32[]{:S(2)}) async-start(), calls=%async_computation.11 | async-start | bytes 2211840 | tf_op jit(solution)/shard_map/all_gather | solution.py:284
  14.3 405.8 %all-gather.33.cloned.1.call-start = ((), (), s32[]{:S(2)}) async-start(), calls=%async_computation.9 | async-start | bytes 1990656 | tf_op jit(solution)/shard_map/all_gather | solution.py:284
  14.9 520.4 %reduce-scatter.19.cloned.1.call-start = ((), (), s32[]{:S(2)}) async-start(), calls=%async_computation.12 | async-start | bytes 1114112
  37.8 152.2 %copy-start.67 = (pred[128,2048]{0,1:T(8,128)(4,1)}, pred[128,2048]{0,1:T(8,128)(4,1)S(1)}, u32[]{:S(2)}) copy-start(pred[128,2048]{0,1:T(8,128)(4,1)S(1)} %broadcast_compare_fusion) | copy-start | bytes 786436
  98.8 91.2 %copy-start.61 = (bf16[2048,192]{0,1:T(8,128)(2,1)}, bf16[2048,192]{0,1:T(8,128)(2,1)S(1)}, u32[]{:S(2)}) copy-start(bf16[2048,192]{0,1:T(8,128)(2,1)S(1)} %all_gather.94) | copy-start | bytes 2359300
  192.4 81.0 %copy-start.66 = (bf16[1,72,576]{2,1,0:T(8,128)(2,1)S(1)}, bf16[1,72,576]{2,1,0:T(8,128)(2,1)}, u32[]{:S(2)}) copy-start(bf16[1,72,576]{2,1,0:T(8,128)(2,1)} %get-tuple-element.66) | copy-start | bytes 248836
  193.7 129.3 %copy-start.79 = (bf16[128,3,64]{0,2,1:T(8,128)(2,1)S(1)}, bf16[128,3,64]{0,2,1:T(8,128)(2,1)}, u32[]{:S(2)}) copy-start(bf16[128,3,64]{0,2,1:T(8,128)(2,1)} %fusion.179) | copy-start | bytes 147460
  193.7 129.3 %copy-start.80 = (bf16[128,3,64]{0,2,1:T(8,128)(2,1)S(1)}, bf16[128,3,64]{0,2,1:T(8,128)(2,1)}, u32[]{:S(2)}) copy-start(bf16[128,3,64]{0,2,1:T(8,128)(2,1)} %fusion.177) | copy-start | bytes 147460
  193.7 129.3 %copy-start.81 = (bf16[128,3,64]{0,2,1:T(8,128)(2,1)S(1)}, bf16[128,3,64]{0,2,1:T(8,128)(2,1)}, u32[]{:S(2)}) copy-start(bf16[128,3,64]{0,2,1:T(8,128)(2,1)} %fusion.178) | copy-start | bytes 147460
  476.0 129.4 %reduce-scatter.21.cloned.1.call-start = ((), (), s32[]{:S(2)}) async-start(), calls=%async_computation.13 | async-start | bytes 1114112
  516.7 306.0 %reduce-scatter.25.cloned.1.call-start = ((), (), s32[]{:S(2)}) async-start(), calls=%async_computation.15 | async-start | bytes 1114112
  624.7 200.3 %reduce-scatter.23.cloned.1.call-start = ((), (), s32[]{:S(2)}) async-start(), calls=%async_computation.14 | async-start | bytes 1114112
  651.2 265.4 %reduce-scatter.29.cloned.1.call-start = ((), (), s32[]{:S(2)}) async-start(), calls=%async_computation.17 | async-start | bytes 7555072
  767.7 258.5 %reduce-scatter.27.cloned.1.call-start = ((), (), s32[]{:S(2)}) async-start(), calls=%async_computation.16 | async-start | bytes 7555072
  916.5 109.7 %copy-start.10 = (bf16[1,1536,576]{2,1,0:T(8,128)(2,1)S(1)}, bf16[1,1536,576]{2,1,0:T(8,128)(2,1)}, u32[]{:S(2)}) copy-start(bf16[1,1536,576]{2,1,0:T(8,128)(2,1)} %all-gather.37.cloned.1.call-done) | copy-start | bytes 5308420
  916.5 109.7 %copy-start.13 = (f32[128,576]{0,1:T(8,128)S(1)}, f32[128,576]{0,1:T(8,128)}, u32[]{:S(2)}) copy-start(f32[128,576]{0,1:T(8,128)} %copy-done.11) | copy-start | bytes 884740
  916.5 109.8 %copy-start.51 = (bf16[128,1536]{1,0:T(8,128)(2,1)S(1)}, bf16[128,1536]{1,0:T(8,128)(2,1)}, u32[]{:S(2)}) copy-start(bf16[128,1536]{1,0:T(8,128)(2,1)} %get-tuple-element.49) | copy-start | bytes 1179652
  916.5 111.2 %copy-start.97 = (f32[128]{0:T(128)S(1)}, f32[128]{0:T(128)}, u32[]{:S(2)}) copy-start(f32[128]{0:T(128)} %copy-done.96) | copy-start | bytes 1540
  916.6 111.2 %copy-start.28 = (f32[128,576]{0,1:T(8,128)S(1)}, f32[128,576]{0,1:T(8,128)}, u32[]{:S(2)}) copy-start(f32[128,576]{0,1:T(8,128)} %copy-done.27) | copy-start | bytes 884740
  916.6 183.8 %all-reduce.12.cloned.1.call-start = ((), (), s32[]{:S(2)}) async-start(), calls=%async_computation.18 | async-start | bytes 1777664
  (88 other events, 971.5 us)
Sparse Core Ops, SparseCore 0:
  10.3 38.6 all-gather.26
  51.3 42.0 all-gather.28
  95.6 42.8 all-gather.30
  140.0 39.6 all-gather.34
  181.7 41.4 all-gather.36
  224.7 41.6 all-gather.32
  476.1 59.1 reduce-scatter.18
  539.6 65.7 reduce-scatter.20
  624.8 65.8 reduce-scatter.24
  694.8 65.7 reduce-scatter.22
  767.9 109.7 reduce-scatter.28
  916.7 109.5 reduce-scatter.26
  1028.8 71.5 all-reduce.11
where the time goes:
time: 1220 us; the launch traced here: 1210 us
  blocking collectives  421 us (35%)
  local copies, waits for them, and re-layouts  294 us (24%)
  waiting for transfers between devices  263 us (22%)
  matrix products  178 us (15%)
  other arithmetic  32.6 us (3%)
  between operations  16.7 us (1%)
    unnamed x20, waiting for transfers between devices  263 us
    all_gather x8, blocking collectives, body(): lax.all_gather(as_sent(pieces), 'dp', axis=0, tiled=True)  201 us
    unnamed x237, local copies, waits for them, and re-layouts  148 us
    all_gather x2, blocking collectives, forward_layer(): lax.all_gather(keys, 'ctx', axis=0, tiled=True)  84.5 us
    all_gather x2, blocking collectives, reduce_grads(): lax.all_gather(piece.astype(jnp.bfloat16), 'ctx', axis=0, tiled=True)  59.8 us
    all_gather x2, blocking collectives, forward_layer(): lax.all_gather(values, 'ctx', axis=0, tiled=True)  57.2 us
    convert_element_type x4, local copies, waits for them, and re-layouts, reduce_grads(): flat.reshape(data_count, context_count, share).astype(jnp.bfloat16)  48.5 us
    dot_general x6, matrix products, backward_layer(): jnp.einsum('jts,tjd->sd', grad_scores, query_group, preferred_element_typ...  40 us
  transfers between devices with their start and end apart: 13, of which 4 were waited for; matrix products, arithmetic and copies ran while one was open for 32% of the time, Pallas kernels for 0%

commit v1 on v0

v1 whole, which is shorter than its diff:
```python
import jax
import jax.numpy as jnp
import numpy as np
from jax import lax
from jax.experimental import pallas as pl
from jax.experimental.pallas import tpu as pltpu
from jax.sharding import PartitionSpec as P

D = 576
HEADS = 9
KV_HEADS = 3
HEAD_DIM = 64
FF = 1536
LAYERS = 2
ROWS = 128
ND = 8
NC = 16
NCHIP = 8
R = 80
PD = 640
MESH = pl.DeviceIdType.MESH
bf16 = jnp.bfloat16
f32 = jnp.float32
NEG = -1e30
eps_norm = 1e-05
rope_base = 100000.0


def nn(a, b):
    return lax.dot_general(a, b, (((1,), (0,)), ((), ())), preferred_element_type=f32)


def nt(a, b):
    return lax.dot_general(a, b, (((1,), (1,)), ((), ())), preferred_element_type=f32)


def tn(a, b):
    return lax.dot_general(a, b, (((0,), (0,)), ((), ())), preferred_element_type=f32)


def kernel(
    hid, gout, cosm, sinm, mlow, e1, e2, gains, wgate, wup, wdown, wattn,
    hout, ghid, ggains, ggate, gup, gdown, gattn,
    land, wd, kvl, dkv, dkr1, dkr2, rs1, rs2, dpb, dpr, fin,
    mid, hs, h1s, apad, bpad, mixp, qc, doc, oT, lse, oz, dqz,
    s1, s2, bias, mk, zpad, gain, acc1, acc2, go4,
    send, recv,
):
    d = lax.axis_index("dp")
    c = lax.axis_index("ctx")
    k = lax.rem(c, 2)
    i = c // 2
    sib = {"ctx": i * 2 + 1 - k}
    count = [0]

    def sems(n):
        count[0] += n
        return count[0] - n

    def dplus(m):
        return lax.rem(d + m, ND)

    def dminus(m):
        return lax.rem(d - m + ND, ND)

    def iplus(m):
        return lax.rem(i + m, NCHIP)

    def iminus(m):
        return lax.rem(i - m + NCHIP, NCHIP)

    def chip(j):
        return {"ctx": j * 2 + k}

    def rc(src, dst, s, dev):
        return pltpu.make_async_remote_copy(
            src_ref=src, dst_ref=dst, send_sem=send.at[s], recv_sem=recv.at[s],
            device_id=dev, device_id_type=MESH,
        )

    def each(f, lo=1, hi=8):
        def step(m, carry):
            f(m)
            return carry
        lax.fori_loop(lo, hi, step, 0)

    def put(l, u, val):
        full = jnp.concatenate([val.astype(f32), jnp.zeros((8, 128), f32)], axis=0)
        land[l, u, d] = full.astype(bf16)

    def pack_attn(l):
        val = wattn[l]
        for t in range(12):
            put(l, 36 + t, val[:, 128 * t:128 * t + 128])
        first = wattn[l, :, 0:128].astype(f32)
        land[l, 36, d] = jnp.concatenate([first, gains[l]], axis=0).astype(bf16)

    def pack_ffn(l):
        for t in range(12):
            put(l, t, wgate[l, :, 128 * t:128 * t + 128])
            put(l, 12 + t, wup[l, :, 128 * t:128 * t + 128])
        for g in range(12):
            for lt in range(5):
                rows = slice(16 * lt, 16 * lt + 16)
                if lt < 4:
                    land[l, 24 + g, d, rows, :] = wdown[l, 16 * g:16 * g + 16, 128 * lt:128 * lt + 128]
                else:
                    land[l, 24 + g, d, rows, :] = jnp.concatenate(
                        [wdown[l, 16 * g:16 * g + 16, 512:576].astype(f32), jnp.zeros((16, 64), f32)], axis=1
                    ).astype(bf16)

    def wref(l, base, n, half, slot):
        return land.at[l, pl.ds(base + n * half, n), slot]

    def w_start(l, base, n, s0):
        def go(m):
            ref = wref(l, base, n, k, d)
            rc(ref, ref, s0 + m - 1, {"dp": dplus(m)}).start()
        each(go)

    def w_forward(l, base, n, s0, s1_):
        def go(m):
            ref = wref(l, base, n, k, dminus(m))
            rc(ref, ref, s0 + m - 1, {"dp": dplus(m)}).wait_recv()
            rc(ref, ref, s1_ + m - 1, sib).start()
        each(go)

    def w_finish(l, base, n, s0, s1_):
        def go(m):
            ref = wref(l, base, n, 1 - k, dminus(m))
            rc(ref, ref, s1_ + m - 1, sib).wait_recv()
            mine = wref(l, base, n, k, dminus(m))
            rc(mine, mine, s1_ + m - 1, sib).wait_send()
            own = wref(l, base, n, k, d)
            rc(own, own, s0 + m - 1, {"dp": dplus(m)}).wait_send()
        each(go)

    wsem = {}
    for l in range(LAYERS):
        for name in ("A", "F"):
            wsem[l, name] = (sems(7), sems(7))
    span = {"A": (36, 6), "F": (0, 18)}

    kv_s = [(sems(7), sems(8)) for _ in range(LAYERS)]

    def kv_start(l):
        own = kvl.at[l, c]
        rc(own, own, kv_s[l][1] + 7, sib).start()
        def go(m):
            rc(own, own, kv_s[l][0] + m - 1, chip(iplus(m))).start()
        each(go)

    def kv_finish(l):
        def go(m):
            ref = kvl.at[l, iminus(m) * 2 + k]
            rc(ref, ref, kv_s[l][0] + m - 1, chip(iplus(m))).wait_recv()
            rc(ref, ref, kv_s[l][1] + m - 1, sib).start()
        each(go)
        own = kvl.at[l, c]
        other = kvl.at[l, i * 2 + 1 - k]
        rc(other, other, kv_s[l][1] + 7, sib).wait_recv()
        rc(own, own, kv_s[l][1] + 7, sib).wait_send()
        def done(m):
            ref = kvl.at[l, iminus(m) * 2 + 1 - k]
            rc(ref, ref, kv_s[l][1] + m - 1, sib).wait_recv()
            mine = kvl.at[l, iminus(m) * 2 + k]
            rc(mine, mine, kv_s[l][1] + m - 1, sib).wait_send()
            rc(own, own, kv_s[l][0] + m - 1, chip(iplus(m))).wait_send()
        each(done)

    dk_s = [(sems(1), sems(7)) for _ in range(LAYERS)]

    def dk_sib(l):
        return rc(dkv.at[:, 1 - k], dkr1.at[l], dk_s[l][0], sib)

    def dk_sum(l):
        def go(j):
            for h in range(KV_HEADS):
                total = dkv[j, k, h].astype(f32) + dkr1[l, j, h].astype(f32)
                dkv[j, k, h] = total.astype(bf16)
        each(go, 0, 8)

    def dk_chip(l, m):
        return rc(dkv.at[iplus(m), k], dkr2.at[l, m - 1], dk_s[l][1] + m - 1, chip(iplus(m)))

    g_s = [((sems(1), sems(7)), (sems(1), sems(7))) for _ in range(LAYERS)]
    gspan = ((0, 16, 2), (32, 8, 1))

    def g_sib(l, q):
        base, n, _ = gspan[q]
        return rc(
            land.at[l, pl.ds(base + n * (1 - k), n)], rs1.at[l, pl.ds(16 * q, n)], g_s[l][q][0], sib
        )

    def g_sum(l, q):
        base, n, _ = gspan[q]
        def go(u):
            total = land[l, base + n * k + u].astype(f32) + rs1[l, 16 * q + u].astype(f32)
            land[l, base + n * k + u] = total.astype(bf16)
        each(go, 0, n)

    def g_chip(l, q, m):
        base, n, per = gspan[q]
        return rc(
            land.at[l, pl.ds(base + n * k + per * iplus(m), per)],
            rs2.at[l, m - 1, pl.ds(2 * q, per)],
            g_s[l][q][1] + m - 1,
            chip(iplus(m)),
        )

    def g_step(l, q):
        g_sib(l, q).wait()
        g_sum(l, q)
        each(lambda m: g_chip(l, q, m).start())

    def g_total(l, q):
        base, n, per = gspan[q]
        each(lambda m: g_chip(l, q, m).wait())
        for s in range(per):
            total = land[l, base + n * k + per * i + s].astype(f32)
            for m in range(7):
                total = total + rs2[l, m, 2 * q + s].astype(f32)
            dpb[:, l, 2 * q + s] = total.astype(bf16)

    dp_s = sems(7)
    ag_s = (sems(7), sems(8))

    barrier = pltpu.get_barrier_semaphore()
    def hello(m):
        pl.semaphore_signal(barrier, inc=1, device_id={"dp": dplus(m)}, device_id_type=MESH)
        pl.semaphore_signal(barrier, inc=1, device_id=chip(iplus(m)), device_id_type=MESH)
    each(hello)
    pl.semaphore_signal(barrier, inc=1, device_id=sib, device_id_type=MESH)
    pack_attn(0)
    pl.semaphore_wait(barrier, 15)
    w_start(0, *span["A"], wsem[0, "A"][0])
    pack_ffn(0)
    w_start(0, *span["F"], wsem[0, "F"][0])
    pack_attn(1)
    w_start(1, *span["A"], wsem[1, "A"][0])
    pack_ffn(1)
    w_start(1, *span["F"], wsem[1, "F"][0])

    lane = lax.broadcasted_iota(jnp.int32, (128, 128), 1)
    low_half = lane < 64
    first_quarter = lax.rem(lane, 64) < 32
    cos_q = cosm[...]
    sin_q = sinm[...]
    cos_kv = jnp.where(low_half, cos_q, 1.0)
    sin_kv = jnp.where(low_half, sin_q, 0.0)

    def swap(x):
        return jnp.where(first_quarter, pltpu.roll(x, 96, axis=1), pltpu.roll(x, 32, axis=1))

    row = lax.broadcasted_iota(jnp.int32, (1024, 192), 0) - 64 * c
    col = lax.rem(lax.broadcasted_iota(jnp.int32, (1024, 192), 1), 64)
    bias[...] = jnp.where((row > col) & (row < 64), NEG, 0.0)
    mk[...] = jnp.concatenate([mlow[...], mlow[:, 0:64]], axis=1).astype(f32)
    row = lax.broadcasted_iota(jnp.int32, (64, 192), 0)
    col = lax.rem(lax.broadcasted_iota(jnp.int32, (64, 192), 1), 64)
    tri = jnp.where(row > col, NEG, 0.0)
    zpad[...] = jnp.zeros((128, PD), bf16)

    def unit(l, u):
        return land[l, u].reshape(PD, 128)

    def pair(l, u):
        return jnp.concatenate([unit(l, u), unit(l, u + 1)], axis=1)

    def units(l, u, n):
        return jnp.concatenate([unit(l, u + j) for j in range(n)], axis=1)

    def norm_scale(h):
        return lax.rsqrt(jnp.mean(h * h, axis=-1, keepdims=True) + eps_norm)

    def spread(x):
        return nn(x.astype(bf16), e1[...]).astype(bf16)

    def unspread(x):
        hi = x.astype(bf16)
        lo = (x - hi.astype(f32)).astype(bf16)
        return nt(hi, e1[...]) + nt(lo, e1[...])

    def load_gains(l):
        total = jnp.zeros((8, PD), f32)
        for s in range(ND):
            part = land[l, 36, s].astype(f32)[72:80, :]
            wide = jnp.concatenate([part, jnp.zeros((8, PD - 128), f32)], axis=1)
            total = total + (pltpu.roll(wide, 72 * s, axis=1) if s else wide)
        gain[l] = total

    def regroup_down(l):
        def go(j):
            src = lax.rem(j, 12)
            for lt in range(5):
                wd[j // 16, pl.ds(pl.multiple_of(lax.rem(j, 16) * 16, 16), 16), 128 * lt:128 * lt + 128] = land[
                    l, 24 + src, j // 12, 16 * lt:16 * lt + 16, :
                ]
        each(go, 0, 96)

    def scatter_down(l):
        def go(j):
            src = lax.rem(j, 12)
            for lt in range(5):
                land[l, 24 + src, j // 12, 16 * lt:16 * lt + 16, :] = wd[
                    j // 16, pl.ds(pl.multiple_of(lax.rem(j, 16) * 16, 16), 16), 128 * lt:128 * lt + 128
                ]
        each(go, 0, 96)

    def tiles(l, h, j):
        tlo = kvl[l, pl.ds(4 * j, 4), h, 0].reshape(256, 128)
        thi = kvl[l, pl.ds(4 * j, 4), h, 1].reshape(256, 128)
        m = mlow[pl.ds(pl.multiple_of(256 * j, 256), 256), :]
        x2 = jnp.concatenate([tlo * m, thi * (1 - m)], axis=1)
        return tlo, x2, m

    def swiglu_parts(l, t, x):
        g = nn(x, pair(l, 2 * t))
        u = nn(x, pair(l, 12 + 2 * t))
        return g, u

    def forward(l, h):
        hs[l] = h
        w_forward(l, *span["A"], *wsem[l, "A"])
        w_finish(l, *span["A"], *wsem[l, "A"])
        load_gains(l)
        apad[l] = spread(h * norm_scale(h) * gain[l, 0:1, 0:D])
        a = apad[l]
        for s in range(KV_HEADS):
            kv = nn(a, unit(l, 45 + s))
            kv = kv * cos_kv + swap(kv) * sin_kv
            kvl[l, c, s] = kv.astype(bf16).reshape(2, 64, 128)
        kv_start(l)
        for t in range(5):
            q = nn(a, unit(l, 40 + t))
            q = (q * cos_q + swap(q) * sin_q) * HEAD_DIM ** (-0.5)
            for j in ((2 * t - 1, 2 * t) if t else (0,)):
                part = q if j % 2 else pltpu.roll(q, 64, axis=1)
                part = jnp.where(low_half, part, 0.0).astype(bf16)
                g = j % 3
                qc[l, j // 3, 64 * g:64 * g + 64, 0:128] = part[0:64]
                qc[l, j // 3, 64 * g:64 * g + 64, 128:256] = part[64:128]
        w_forward(l, *span["F"], *wsem[l, "F"])
        kv_finish(l)

        def head(s):
            qcat = qc[l, s]
            qT = qcat.astype(f32).T.astype(bf16)
            qhT = qT[128:256]
            top_own = kvl[l, c, s, 1]
            se = nn(top_own, qhT) + tri

            def scores(j, carry):
                ml, mh = carry
                tlo, x2, _ = tiles(l, s, j)
                at = pl.ds(pl.multiple_of(256 * j, 256), 256)
                a1 = nn(tlo, qhT)
                a2 = nn(x2, qT) + bias[at, :]
                s1[at, 0:192] = a1
                s2[at, 0:192] = a2
                is_low = mk[at, :] > 0.5
                ml = jnp.maximum(ml, jnp.max(jnp.where(is_low, a2, NEG), axis=0, keepdims=True))
                mh = jnp.maximum(
                    mh, jnp.max(jnp.maximum(a1, jnp.where(is_low, NEG, a2)), axis=0, keepdims=True)
                )
                return ml, mh

            ml, mh = lax.fori_loop(
                0, 4, scores,
                (jnp.full((1, 192), NEG, f32), jnp.max(se, axis=0, keepdims=True)),
            )
            pe = jnp.exp(se - mh)
            acc1[...] = tn(top_own, pe.astype(bf16))
            acc2[...] = jnp.zeros((256, 192), f32)

            def weigh(j, carry):
                ll, lh = carry
                tlo, x2, _ = tiles(l, s, j)
                at = pl.ds(pl.multiple_of(256 * j, 256), 256)
                is_low = mk[at, :] > 0.5
                p1 = jnp.exp(s1[at, 0:192] - mh)
                p2 = jnp.exp(s2[at, 0:192] - jnp.where(is_low, ml, mh))
                ll = ll + jnp.sum(jnp.where(is_low, p2, 0.0), axis=0, keepdims=True)
                lh = lh + jnp.sum(p1 + jnp.where(is_low, 0.0, p2), axis=0, keepdims=True)
                acc1[...] += tn(tlo, p1.astype(bf16))
                acc2[...] += tn(x2, p2.astype(bf16))
                return ll, lh

            ll, lh = lax.fori_loop(
                0, 4, weigh, (jnp.zeros((1, 192), f32), jnp.sum(pe, axis=0, keepdims=True))
            )
            olow = acc2[64:128, :] / ll
            ohigh = (acc2[192:256, :] + acc1[64:128, :]) / lh
            oT[l, s, 0:64, :] = olow
            oT[l, s, 64:128, :] = ohigh
            lse[l, s, 0:1, :] = ml + jnp.log(ll)
            lse[l, s, 1:2, :] = mh + jnp.log(lh)
            zero = jnp.zeros((64, 192), f32)
            tl = jnp.concatenate([zero, olow], axis=0).T.astype(bf16)
            th = jnp.concatenate([zero, ohigh], axis=0).T.astype(bf16)
            for g in range(3):
                oz[3 * s + g, 0:64, :] = tl[64 * g:64 * g + 64]
                oz[3 * s + g, 64:128, :] = th[64 * g:64 * g + 64]

        each(head, 0, KV_HEADS)
        mixp[l] = nt(jnp.concatenate([oz[j] for j in range(HEADS)], axis=1), e2[...]).astype(bf16)
        y = nn(mixp[l], units(l, 36, 5))
        h1 = h + y[:, 0:D]
        h1s[l] = h1
        bpad[l] = spread(h1 * norm_scale(h1) * gain[l, 1:2, 0:D])
        w_finish(l, *span["F"], *wsem[l, "F"])
        regroup_down(l)

        def ffn(t, total):
            g, u = swiglu_parts(l, t, bpad[l])
            if l == LAYERS - 1:
                s1[pl.ds(pl.multiple_of(128 * t, 128), 128), :] = g
                s2[pl.ds(pl.multiple_of(128 * t, 128), 128), :] = u
            m = (g / (1.0 + jnp.exp(-g)) * u).astype(bf16)
            mid[l, t] = m
            return total + nn(m, wd[t])

        total = lax.fori_loop(0, 6, ffn, jnp.zeros((128, PD), f32))
        return h1 + total[:, 0:D]

    def norm_back(h, g, dn, gain_row):
        r = norm_scale(h)
        xn = h * r
        cc = dn * gain_row
        return (
            g + r * (cc - xn * jnp.mean(cc * xn, axis=-1, keepdims=True)),
            jnp.sum(dn * xn, axis=0, keepdims=True),
        )

    def backward(l, g):
        zpad[:, 0:D] = g.astype(bf16)
        if l < LAYERS - 1:
            regroup_down(l)
        bT = bpad[l].T

        def ffn(t, total):
            dz = zpad[...]
            if l == LAYERS - 1:
                at = pl.ds(pl.multiple_of(128 * t, 128), 128)
                ga, u = s1[at, :], s2[at, :]
            else:
                ga, u = swiglu_parts(l, t, bpad[l])
            dm = nt(dz, wd[t])
            sg = 1.0 / (1.0 + jnp.exp(-ga))
            silu = ga * sg
            dg = (dm * u * (sg * (1.0 + ga * (1.0 - sg)))).astype(bf16)
            du = (dm * silu).astype(bf16)
            total = total + nt(dg, pair(l, 2 * t)) + nt(du, pair(l, 12 + 2 * t))
            wd[t] = tn(mid[l, t], dz).astype(bf16)
            gw = nn(bT, dg).astype(bf16)
            land[l, 2 * t] = gw[:, 0:128].reshape(8, R, 128)
            land[l, 2 * t + 1] = gw[:, 128:256].reshape(8, R, 128)
            gw = nn(bT, du).astype(bf16)
            land[l, 12 + 2 * t] = gw[:, 0:128].reshape(8, R, 128)
            land[l, 13 + 2 * t] = gw[:, 128:256].reshape(8, R, 128)
            return total

        total = lax.fori_loop(0, 6, ffn, jnp.zeros((128, PD), f32))
        scatter_down(l)
        g_sib(l, 0).start()
        if l < LAYERS - 1:
            g_step(l + 1, 1)
        dh1, dgain_ffn = norm_back(h1s[l], g, unspread(total), gain[l, 1:2, 0:D])
        zpad[:, 0:D] = dh1.astype(bf16)
        do = nt(zpad[...], units(l, 36, 5)).astype(bf16)
        go = nn(mixp[l].T, zpad[...]).astype(bf16)
        for t in range(4):
            land[l, 36 + t] = go[:, 128 * t:128 * t + 128].reshape(8, R, 128)
        go4[...] = go[:, 512:640]
        for j in range(HEADS):
            part = nn(do, e2[:, 128 * j:128 * j + 128]).astype(bf16)
            gidx = j % 3
            doc[j // 3, 64 * gidx:64 * gidx + 64, 0:128] = part[0:64]
            doc[j // 3, 64 * gidx:64 * gidx + 64, 128:256] = part[64:128]

        def head(s):
            qcat = qc[l, s]
            qh = qcat[:, 128:256]
            qT = qcat.astype(f32).T.astype(bf16)
            qhT = qT[128:256]
            docat = doc[s]
            doh = docat[:, 128:256]
            doT = docat.astype(f32).T
            doTb = doT.astype(bf16)
            dohT = doTb[128:256]
            dl = jnp.sum(oT[l, s, 0:64, :] * doT[64:128, :], axis=0, keepdims=True)
            dh = jnp.sum(oT[l, s, 64:128, :] * doT[192:256, :], axis=0, keepdims=True)
            lsl = lse[l, s, 0:1, :]
            lsh = lse[l, s, 1:2, :]
            own = kvl[l, c, s, 1]
            pe = jnp.exp(nn(own, qhT) + tri - lsh)
            dse = (pe * (nn(own, dohT) - dh)).astype(bf16)
            dxe = nn(dse, qh) + nn(pe.astype(bf16), doh)
            acc1[...] = tn(own, dse)
            acc2[...] = jnp.zeros((256, 192), f32)

            def chunk(j):
                tlo, x2, m = tiles(l, s, j)
                at = pl.ds(pl.multiple_of(256 * j, 256), 256)
                is_low = mk[at, :] > 0.5
                p1 = jnp.exp(nn(tlo, qhT) - lsh)
                p2 = jnp.exp(nn(x2, qT) + bias[at, :] - jnp.where(is_low, lsl, lsh))
                ds1 = (p1 * (nn(tlo, dohT) - dh)).astype(bf16)
                ds2 = (p2 * (nn(x2, doTb) - jnp.where(is_low, dl, dh))).astype(bf16)
                p1 = p1.astype(bf16)
                p2 = p2.astype(bf16)
                dx1 = nn(ds1, qh) + nn(p1, doh)
                dx2 = nn(ds2, qcat) + nn(p2, docat)
                mf = m.astype(f32)
                lo = dx1 + mf * dx2[:, 0:128]
                hi = (1.0 - mf) * dx2[:, 128:256]
                dkv[pl.ds(2 * j, 2), :, s, 0] = lo.astype(bf16).reshape(2, 2, 64, 128)
                dkv[pl.ds(2 * j, 2), :, s, 1] = hi.astype(bf16).reshape(2, 2, 64, 128)
                acc1[...] += tn(tlo, ds1)
                acc2[...] += tn(x2, ds2)

            each(chunk, 0, 4)
            dkv[i, k, s, 1] = dxe.astype(bf16)
            zero = jnp.zeros((64, 192), f32)
            tl = jnp.concatenate([acc2[0:64, :], zero], axis=0).T
            th = jnp.concatenate([acc2[128:192, :] + acc1[0:64, :], zero], axis=0).T
            scale = HEAD_DIM ** (-0.5)
            for gidx in range(3):
                dqz[3 * s + gidx, 0:64, :] = tl[64 * gidx:64 * gidx + 64] * scale
                dqz[3 * s + gidx, 64:128, :] = th[64 * gidx:64 * gidx + 64] * scale

        each(head, 0, KV_HEADS)
        dk_sib(l).start()
        g_step(l, 0)
        dk_sib(l).wait()
        dk_sum(l)
        each(lambda m: dk_chip(l, m).start())

        rot = []
        for j in range(HEADS):
            x = dqz[j]
            rot.append(x * cos_q - swap(x) * sin_q)
        dq = [pltpu.roll(rot[0], 64, axis=1).astype(bf16)]
        for t in range(1, 5):
            dq.append((rot[2 * t - 1] + pltpu.roll(rot[2 * t], 64, axis=1)).astype(bf16))
        dq = jnp.concatenate(dq, axis=1)
        aT = apad[l].T

        each(lambda m: dk_chip(l, m).wait())
        dkv_in = []
        for s in range(KV_HEADS):
            x = dkv[i, k, s].astype(f32)
            for m in range(7):
                x = x + dkr2[l, m, s].astype(f32)
            x = x.reshape(128, 128)
            dkv_in.append((x * cos_kv - swap(x) * sin_kv).astype(bf16))
        dkv_in = jnp.concatenate(dkv_in, axis=1)
        da = nt(dq, units(l, 40, 5)) + nt(dkv_in, units(l, 45, 3))
        gq = nn(aT, dq).astype(bf16)
        land[l, 40] = (gq[:, 0:128] + go4[...]).reshape(8, R, 128)
        for t in range(1, 5):
            land[l, 40 + t] = gq[:, 128 * t:128 * t + 128].reshape(8, R, 128)
        gkv = nn(aT, dkv_in).astype(bf16)
        for t in range(3):
            land[l, 45 + t] = gkv[:, 128 * t:128 * t + 128].reshape(8, R, 128)
        dh, dgain_attn = norm_back(hs[l], dh1, unspread(da), gain[l, 0:1, 0:D])
        rows = jnp.concatenate([dgain_attn, dgain_ffn, jnp.zeros((6, D), f32)], axis=0)
        rows = jnp.concatenate([rows, jnp.zeros((8, PD - D), f32)], axis=1)
        for s in range(ND):
            part = (pltpu.roll(rows, PD - 72 * s, axis=1) if s else rows)[:, 0:128]
            keep = land[l, 36, s].astype(f32)[0:72, :]
            land[l, 36, s] = jnp.concatenate([keep, part], axis=0).astype(bf16)
        g_sib(l, 1).start()
        return dh

    h = hid[...].astype(f32)
    h = forward(0, h)
    h = forward(1, h)
    hout[...] = h.astype(bf16)
    g = backward(1, gout[...].astype(f32))
    g = backward(0, g)
    ghid[...] = g
    g_step(0, 1)
    g_total(1, 0)
    g_total(1, 1)
    g_total(0, 0)
    g_total(0, 1)

    def dp_copy(m):
        return rc(dpb.at[dplus(m)], dpr.at[m - 1], dp_s + m - 1, {"dp": dplus(m)})
    each(lambda m: dp_copy(m).start())
    each(lambda m: dp_copy(m).wait())
    for l in range(LAYERS):
        for s in range(3):
            total = dpb[d, l, s].astype(f32)
            for m in range(7):
                total = total + dpr[m, l, s].astype(f32)
            fin[c, l, s] = total.astype(bf16)
    own = fin.at[c]
    rc(own, own, ag_s[1] + 7, sib).start()
    each(lambda m: rc(own, own, ag_s[0] + m - 1, chip(iplus(m))).start())
    def pass_on(m):
        ref = fin.at[iminus(m) * 2 + k]
        rc(ref, ref, ag_s[0] + m - 1, chip(iplus(m))).wait_recv()
        rc(ref, ref, ag_s[1] + m - 1, sib).start()
    each(pass_on)
    other = fin.at[i * 2 + 1 - k]
    rc(other, other, ag_s[1] + 7, sib).wait_recv()
    rc(own, own, ag_s[1] + 7, sib).wait_send()
    def done(m):
        ref = fin.at[iminus(m) * 2 + 1 - k]
        rc(ref, ref, ag_s[1] + m - 1, sib).wait_recv()
        mine = fin.at[iminus(m) * 2 + k]
        rc(mine, mine, ag_s[1] + m - 1, sib).wait_send()
        rc(own, own, ag_s[0] + m - 1, chip(iplus(m))).wait_send()
    each(done)

    for l in range(LAYERS):
        for cc in range(NC):
            ii, kk = cc // 2, cc % 2
            for s, u in enumerate((16 * kk + 2 * ii, 16 * kk + 2 * ii + 1, 32 + 8 * kk + ii)):
                val = fin[cc, l, s].astype(f32)
                if u < 12:
                    ggate[l, :, 128 * u:128 * u + 128] = val[0:72]
                elif u < 24:
                    gup[l, :, 128 * (u - 12):128 * (u - 12) + 128] = val[0:72]
                elif u < 36:
                    at = slice(16 * (u - 24), 16 * (u - 24) + 16)
                    for lt in range(4):
                        gdown[l, at, 128 * lt:128 * lt + 128] = val[16 * lt:16 * lt + 16]
                    gdown[l, at, 512:576] = val[64:80, 0:64]
                else:
                    gattn[l, :, 128 * (u - 36):128 * (u - 36) + 128] = val[0:72]
                    if u == 36:
                        ggains[l] = val[72:80]


def body(
    hidden_in, positions, attn_gain, w_query, w_key, w_value, w_output, ffn_gain, w_gate, w_up, w_down, grad_out
):
    own = lax.dynamic_slice_in_dim(positions, lax.axis_index("ctx") * ROWS, ROWS)
    half = HEAD_DIM // 2
    freq = jnp.exp(-jnp.log(rope_base) * (2.0 * jnp.arange(half, dtype=f32) / HEAD_DIM))
    angle = own.astype(f32)[:, None] * jnp.tile(freq, 4)[None, :]
    sign = jnp.tile(jnp.where(jnp.arange(HEAD_DIM) < half, -1.0, 1.0), 2).astype(f32)
    cosm, sinm = jnp.cos(angle), jnp.sin(angle) * sign[None, :]
    low = (positions.reshape(NC, ROWS)[:, 0] <= own[0]).astype(bf16)
    mlow = jnp.broadcast_to(low[:, None, None], (NC, 64, 128)).reshape(NC * 64, 128)
    spread = np.zeros((D, PD), np.float32)
    for s in range(ND):
        spread[72 * s + np.arange(72), R * s + np.arange(72)] = 1
    heads = np.zeros((PD, 128 * HEADS), np.float32)
    for t in range(D):
        heads[R * (t // 72) + t % 72, 128 * (t // 64) + 64 + t % 64] = 1
    gains = jnp.stack([attn_gain, ffn_gain], axis=1).astype(f32)
    gains = jnp.pad(gains, ((0, 0), (0, 6), (0, 56)))
    kv = jnp.stack(
        [w_key.reshape(LAYERS, 72, KV_HEADS, HEAD_DIM), w_value.reshape(LAYERS, 72, KV_HEADS, HEAD_DIM)], axis=3
    ).reshape(LAYERS, 72, 2 * KV_HEADS * HEAD_DIM)
    wattn = jnp.concatenate([w_output, w_query, kv], axis=2)
    outs = pl.pallas_call(
        kernel,
        out_shape=(
            jax.ShapeDtypeStruct((ROWS, D), bf16),
            jax.ShapeDtypeStruct((ROWS, D), f32),
            jax.ShapeDtypeStruct((LAYERS, 8, 128), f32),
            jax.ShapeDtypeStruct((LAYERS, 72, FF), f32),
            jax.ShapeDtypeStruct((LAYERS, 72, FF), f32),
            jax.ShapeDtypeStruct((LAYERS, 192, D), f32),
            jax.ShapeDtypeStruct((LAYERS, 72, FF), f32),
        ),
        in_specs=[pl.BlockSpec(memory_space=pltpu.VMEM)] * 12,
        out_specs=tuple([pl.BlockSpec(memory_space=pltpu.VMEM)] * 7),
        scratch_shapes=[
            pltpu.VMEM((LAYERS, 48, ND, R, 128), bf16),
            pltpu.VMEM((6, 256, PD), bf16),
            pltpu.VMEM((LAYERS, NC, KV_HEADS, 2, 64, 128), bf16),
            pltpu.VMEM((NCHIP, 2, KV_HEADS, 2, 64, 128), bf16),
            pltpu.VMEM((LAYERS, NCHIP, KV_HEADS, 2, 64, 128), bf16),
            pltpu.VMEM((LAYERS, 7, KV_HEADS, 2, 64, 128), bf16),
            pltpu.VMEM((LAYERS, 24, ND, R, 128), bf16),
            pltpu.VMEM((LAYERS, 7, 3, ND, R, 128), bf16),
            pltpu.VMEM((ND, LAYERS, 3, R, 128), bf16),
            pltpu.VMEM((7, LAYERS, 3, R, 128), bf16),
            pltpu.VMEM((NC, LAYERS, 3, R, 128), bf16),
            pltpu.VMEM((LAYERS, 6, 128, 256), bf16),
            pltpu.VMEM((LAYERS, 128, D), f32),
            pltpu.VMEM((LAYERS, 128, D), f32),
            pltpu.VMEM((LAYERS, 128, PD), bf16),
            pltpu.VMEM((LAYERS, 128, PD), bf16),
            pltpu.VMEM((LAYERS, 128, PD), bf16),
            pltpu.VMEM((LAYERS, KV_HEADS, 192, 256), bf16),
            pltpu.VMEM((KV_HEADS, 192, 256), bf16),
            pltpu.VMEM((LAYERS, KV_HEADS, 128, 192), f32),
            pltpu.VMEM((LAYERS, KV_HEADS, 8, 192), f32),
            pltpu.VMEM((HEADS, 128, 128), bf16),
            pltpu.VMEM((HEADS, 128, 128), f32),
            pltpu.VMEM((1024, 256), f32),
            pltpu.VMEM((1024, 256), f32),
            pltpu.VMEM((1024, 192), f32),
            pltpu.VMEM((1024, 192), f32),
            pltpu.VMEM((128, PD), bf16),
            pltpu.VMEM((LAYERS, 8, PD), f32),
            pltpu.VMEM((128, 192), f32),
            pltpu.VMEM((256, 192), f32),
            pltpu.VMEM((PD, 128), bf16),
            pltpu.SemaphoreType.DMA((192,)),
            pltpu.SemaphoreType.DMA((192,)),
        ],
        compiler_params=pltpu.CompilerParams(
            collective_id=0, has_side_effects=True, vmem_limit_bytes=63 * 1024 * 1024
        ),
    )(
        hidden_in, grad_out, cosm, sinm, mlow, jnp.asarray(spread, bf16), jnp.asarray(heads, bf16), gains,
        w_gate, w_up, w_down, wattn,
    )
    hout, ghid, ggains, ggate, gup, gdown, gattn = outs
    gkv = gattn[:, :, 2 * D:].reshape(LAYERS, 72, KV_HEADS, 2, HEAD_DIM)
    return (
        hout,
        ghid,
        ggains[:, 0, 0:72],
        gattn[:, :, D:2 * D],
        gkv[:, :, :, 0].reshape(LAYERS, 72, KV_HEADS * HEAD_DIM),
        gkv[:, :, :, 1].reshape(LAYERS, 72, KV_HEADS * HEAD_DIM),
        gattn[:, :, 0:D],
        ggains[:, 1, 0:72],
        ggate,
        gup,
        gdown,
    )


def solution(mesh):
    placed = (
        P(("dp", "ctx"), None),
        P("dp"),
        P(None, "dp"),
        P(None, "dp", None),
        P(None, "dp", None),
        P(None, "dp", None),
        P(None, "dp", None),
        P(None, "dp"),
        P(None, "dp", None),
        P(None, "dp", None),
        P(None, "dp", None),
        P(("dp", "ctx"), None),
    )
    out = (
        P(("dp", "ctx"), None),
        P(("dp", "ctx"), None),
        P(None, "dp"),
        P(None, "dp", None),
        P(None, "dp", None),
        P(None, "dp", None),
        P(None, "dp", None),
        P(None, "dp"),
        P(None, "dp", None),
        P(None, "dp", None),
        P(None, "dp", None),
    )
    return jax.shard_map(body, mesh=mesh, in_specs=placed, out_specs=out, check_vma=False)
```

time: 1220 us -> 381 us (0.31)
  blocking collectives: 421 us -> 0 us
  Pallas kernels: 0 us -> 355 us
  local copies, waits for them, and re-layouts: 294 us -> 19.7 us
  waiting for transfers between devices: 263 us -> 0 us
  matrix products: 178 us -> 0 us
  other arithmetic: 32.6 us -> 3.4 us
  between operations: 16.7 us -> 0.79 us
    all_gather x14 -> x0, blocking collectives: 403 us -> none  [the longest x8 201 us: body(): lax.all_gather(as_sent(pieces), 'dp', axis=0, tiled=True)]
    pallas_call x0 -> x1, Pallas kernels: none -> 355 us  [body(): pl.pallas_call(kernel, out_shape=(jax.ShapeDtypeStruct((ROWS, D), bf16),...]
    unnamed x20 -> x0, waiting for transfers between devices: 263 us -> none
    dot_general x78 -> x0, matrix products: 178 us -> none  [the longest x6 40 us: backward_layer(): jnp.einsum('jts,tjd->sd', grad_scores, query_group, preferred_element_typ...]
    unnamed x237 -> x27, local copies, waits for them, and re-layouts: 148 us -> 10.6 us
    convert_element_type x4 -> x0, local copies, waits for them, and re-layouts: 48.5 us -> none  [reduce_grads(): flat.reshape(data_count, context_count, share).astype(jnp.bfloat16)]
    reshape x20 -> x2, local copies, waits for them, and re-layouts: 37.5 us -> 0.49 us  [the longest x1 0.29 us: body(): gkv = gattn[:, :, 2 * D:].reshape(LAYERS, 72, KV_HEADS, 2, HEAD_DIM)]
    another operation x22 -> x5, local copies, waits for them, and re-layouts: 24.3 us -> 1.48 us  [the longest x2 1.32 us: body(): gains = jnp.stack([attn_gain, ffn_gain], axis=1).astype(f32)]
  transfers between devices with their start and end apart: 13 -> 0, of which waited for: 4 -> 0; matrix products, arithmetic and copies ran while one was open for 32% -> 0% of each run, Pallas kernels for 0% -> 0%
where the time goes in v1:
time: 381 us; the launch traced here: 379 us
  Pallas kernels  355 us (93%)
  local copies, waits for them, and re-layouts  19.7 us (5%)
    pallas_call x1, Pallas kernels, body(): pl.pallas_call(kernel, out_shape=(jax.ShapeDtypeStruct((ROWS, D), bf16),...  355 us
    unnamed x27, local copies, waits for them, and re-layouts  10.6 us

profile of v1, /device:TPU:1, one launch (start us, length us, event | category | flops | bytes accessed | tf_op | source)
XLA Modules:
  0.0 379.3 jit_solution(16371295291134427753)
XLA Ops:
  0.8 0.9 fusion.10
  1.7 0.8 fusion.9
  2.6 0.7 copy.44
  3.2 0.7 copy.45
  4.1 0.6 fusion.8.gains
  4.7 1.0 copy.46
  5.7 1.0 copy.47
  7.2 1.0 fusion
  8.1 0.8 copy.49.hid
  9.0 0.8 copy.50.gout
  9.8 0.9 broadcast_in_dim.23.mlow
  10.7 0.9 concatenate.3.wattn
  11.6 355.4 %shard_map.221 = (bf16[128,576]{1,0:T(8,128)(2,1)}, f32[128,576]{1,0:T(8,128)}, f32[2,8,128]{2,1,0:T(8,128)}, f32[2,72,1536]{2,1,0:T(8,128)}, f32[2,72,1536]{2,1...) custom-call(bf16[128,576]{1,0:T(8,128)(2,1)} %copy.49.hid, bf16[128,576]{1,0:T(8,128)(2,1)} %copy.50.gout, ...), custom_call_target="tpu_custom_call" | custom-call | tf_op jit(solution)/shard_map/pallas_call | solution.py:661
  367.0 1.7 copy.53
  368.7 1.3 fusion.13
  370.1 1.0 slice.31
  371.0 2.1 fusion.11
  373.4 0.3 fusion.12
  373.9 0.8 copy.56
  374.8 0.8 copy.55
  375.6 0.9 copy.54
  376.5 0.9 copy.60
  377.4 0.9 copy.61
  378.3 0.9 copy.62
  (30 shorter events, 1.3 us)
Async XLA Ops:
  0.6 8.3 %copy-start.7 = (bf16[128,576]{0,1:T(8,128)(2,1)S(1)}, bf16[128,576]{0,1:T(8,128)(2,1)}, u32[]{:S(2)}) copy-start(bf16[128,576]{0,1:T(8,128)(2,1)} %param.25) | copy-start | bytes 442372
  0.7 10.0 %copy-start.4 = (bf16[2,72,576]{2,1,0:T(8,128)(2,1)S(1)}, bf16[2,72,576]{2,1,0:T(8,128)(2,1)}, u32[]{:S(2)}) copy-start(bf16[2,72,576]{2,1,0:T(8,128)(2,1)} %param.20) | copy-start | bytes 497668
  0.7 10.0 %copy-start.5 = (bf16[2,72,576]{2,1,0:T(8,128)(2,1)S(1)}, bf16[2,72,576]{2,1,0:T(8,128)(2,1)}, u32[]{:S(2)}) copy-start(bf16[2,72,576]{2,1,0:T(8,128)(2,1)} %param.17) | copy-start | bytes 497668
  0.7 7.5 %copy-start.6 = (bf16[128,576]{0,1:T(8,128)(2,1)S(1)}, bf16[128,576]{0,1:T(8,128)(2,1)}, u32[]{:S(2)}) copy-start(bf16[128,576]{0,1:T(8,128)(2,1)} %param.14) | copy-start | bytes 442372
  373.1 2.5 copy-start.3
  373.4 3.1 copy-start.2
  374.7 2.7 copy-start.1
  376.5 1.8 copy-start

commit v2 on v1

v2 whole, which is shorter than its diff:
```python
import jax
import jax.numpy as jnp
import numpy as np
from jax import lax
from jax.experimental import pallas as pl
from jax.experimental.pallas import tpu as pltpu
from jax.sharding import PartitionSpec as P

D = 576
HEADS = 9
KV_HEADS = 3
HEAD_DIM = 64
FF = 1536
LAYERS = 2
ROWS = 128
ND = 8
NC = 16
NCHIP = 8
R = 80
PD = 640
MESH = pl.DeviceIdType.MESH
bf16 = jnp.bfloat16
f32 = jnp.float32
NEG = -1e30
eps_norm = 1e-05
rope_base = 100000.0


def nn(a, b):
    return lax.dot_general(a, b, (((1,), (0,)), ((), ())), preferred_element_type=f32)


def nt(a, b):
    return lax.dot_general(a, b, (((1,), (1,)), ((), ())), preferred_element_type=f32)


def tn(a, b):
    return lax.dot_general(a, b, (((0,), (0,)), ((), ())), preferred_element_type=f32)


class Move:
    def __init__(self, make, src, dst, inc, s, dev):
        self.out = lambda: make(src, dst, s, dev)
        self.inc = lambda: make(inc, inc, s, dev)

    def start(self):
        self.out().start()

    def recv(self):
        self.inc().wait_recv()

    def sent(self):
        self.out().wait_send()


def kernel(
    hid, gout, cosm, sinm, mlow, e1, e2, gains, wgate, wup, wdown, wattn,
    hout, ghid, ggains, ggate, gup, gdown, gattn,
    land, wd, kvl, dkv, dkr0, dkr1,
    rs0, r1e, rz, r2e, r1l, r2l, fine, finl,
    mid, hs, h1s, apad, bpad, mixp, qc, doc, oT, lse, oz, dqz,
    s1, s2, bias, mk, zpad, gain, acc1, acc2, go4,
    send, recv,
):
    d = lax.axis_index("dp")
    c = lax.axis_index("ctx")
    k, y = lax.rem(c, 2), lax.rem(c // 2, 4)
    x, zl = lax.rem(d, 4), d // 4
    i = c // 2
    sib = {"ctx": i * 2 + 1 - k}
    count = [0]

    def dplus(m):
        return lax.rem(d + m, ND)

    def dminus(m):
        return lax.rem(d - m + ND, ND)

    def iplus(m):
        return lax.rem(i + m, NCHIP)

    def iminus(m):
        return lax.rem(i - m + NCHIP, NCHIP)

    def shard(m):
        return {"dp": dplus(m)}

    def chip(m):
        return {"ctx": iplus(m) * 2 + k}

    def near(at, o):
        return lax.rem(at + o + 4, 4)

    def Y(o):
        return {"ctx": ((i // 4) * 4 + near(y, o)) * 2 + k}

    def rc(src, dst, s, to):
        return pltpu.make_async_remote_copy(
            src_ref=src, dst_ref=dst, send_sem=send.at[s], recv_sem=recv.at[s],
            device_id=to, device_id_type=MESH,
        )

    def sems(n):
        count[0] += n
        return count[0] - n

    def move(src, dst, inc, to, s=None):
        return Move(rc, src, dst, inc, sems(1) if s is None else s, to)

    def starts(*moves):
        for m in moves:
            m.start()

    def recvs(*moves):
        for m in moves:
            m.recv()

    def sents(*moves):
        for m in moves:
            m.sent()

    def each(f, lo=1, hi=8):
        def step(m, carry):
            f(m)
            return carry
        lax.fori_loop(lo, hi, step, 0)

    def put(l, j, val, last=None, k=k):
        last = jnp.zeros((8, 128), f32) if last is None else last
        land[l, k, j, d] = jnp.concatenate([val.astype(f32), last], axis=0).astype(bf16)

    def column(t):
        return pl.ds(pl.multiple_of(128 * t, 128), 128)

    def pack_attn(l):
        if l == 0:
            for t in range(12):
                put(l, 18 + t % 6, wattn[l, :, 128 * t:128 * t + 128], gains[l], t // 6)
        else:
            put(l, 18 + y, wattn[l, :, column(6 * k + y)], gains[l])
            put(l, 22, wattn[l, :, column(6 * k + 4)])
            put(l, 23, wattn[l, :, column(6 * k + 5)])

    def pack_ffn(l):
        @pl.when(y < 2)
        def _():
            for r in range(3):
                put(l, 3 * y + r, wgate[l, :, column(6 * k + 3 * y + r)])

        @pl.when(y >= 2)
        def _():
            for r in range(3):
                put(l, 3 * y + r, wup[l, :, column(6 * k + 3 * (y - 2) + r)])

        for g in range(6):
            val = wdown[l, pl.ds(pl.multiple_of(16 * (6 * k + g), 16), 16), :]
            val = jnp.concatenate([val.astype(f32), jnp.zeros((16, 64), f32)], axis=1).astype(bf16)
            for lt in range(5):
                land[l, k, 12 + g, d, 16 * lt:16 * lt + 16, :] = val[:, 128 * lt:128 * lt + 128]

    class Weights:
        def __init__(self, l, shared, direct):
            self.shared = shared is not None
            db, nd = direct

            def straight(slot):
                return land.at[l, k, pl.ds(db, nd), slot]

            self.parts = [(straight, sems(7))]
            here, there = land.at[l, k, pl.ds(db, nd)], land.at[l, 1 - k, pl.ds(db, nd)]
            self.u = []
            if not self.shared:
                self.v = None
                self.base = sems(7)
                self.slot = lambda k_, slot: land.at[l, k_, pl.ds(db, nd), slot]
                return
            sb, ns = shared
            self.parts.append((lambda slot: land.at[l, k, pl.ds(sb + ns * y, ns), slot], sems(7)))
            self.v = [move(here, here, there, sib)]

            def block(y_, k_=k, half=None):
                ref = land.at[l, k_, pl.ds(sb + ns * y_, ns)]
                return ref if half is None else ref.at[:, pl.ds(4 * half, 4)]

            yp, ym, y2 = near(y, 1), near(y, -1), near(y, 2)
            self.u = [
                move(block(y), block(y), block(ym), Y(1)), move(block(y), block(y), block(yp), Y(-1)),
                move(block(ym, half=0), block(ym, half=0), block(y2, half=0), Y(1)),
                move(block(yp, half=1), block(yp, half=1), block(y2, half=1), Y(-1)),
            ]
            self.v += [move(block(y_), block(y_), block(y_, 1 - k), sib) for y_ in (y, ym, yp, y2)]

        def one(self, part):
            ref, s = self.parts[part]
            each(lambda m: rc(ref(d), ref(d), s + m - 1, shard(m)).start())

        def two(self):
            def go(m):
                for ref, s in self.parts:
                    own = ref(dminus(m))
                    rc(own, own, s + m - 1, shard(m)).wait_recv()
                    if not self.shared:
                        rc(own, own, self.base + m - 1, sib).start()
            each(go)
            if self.shared:
                starts(self.u[0], self.u[1], self.v[0], self.v[1])

        def three(self):
            recvs(self.u[0])
            starts(self.u[2], self.v[2])
            recvs(self.u[1])
            starts(self.u[3], self.v[3])

        def four(self):
            recvs(self.u[2], self.u[3])
            starts(self.v[4])

        def five(self):
            if self.shared:
                recvs(*self.v)
                sents(*self.u)
                sents(*self.v)

            def go(m):
                for ref, s in self.parts:
                    rc(ref(d), ref(d), s + m - 1, shard(m)).wait_send()
                if not self.shared:
                    got, gave = self.slot(1 - k, dminus(m)), self.slot(k, dminus(m))
                    rc(got, got, self.base + m - 1, sib).wait_recv()
                    rc(gave, gave, self.base + m - 1, sib).wait_send()
            each(go)

    class Keys:
        def __init__(self, l):
            self.l, self.a, self.b = l, sems(7), sems(7)
            own = kvl.at[l, i, k]
            self.s = move(own, own, kvl.at[l, i, 1 - k], sib)

        def one(self):
            own = kvl.at[self.l, i, k]
            each(lambda m: rc(own, own, self.a + m - 1, chip(m)).start())
            starts(self.s)

        def two(self):
            def go(m):
                ref = kvl.at[self.l, iminus(m), k]
                rc(ref, ref, self.a + m - 1, chip(m)).wait_recv()
                rc(ref, ref, self.b + m - 1, sib).start()
            each(go)

        def three(self):
            recvs(self.s)
            sents(self.s)

            def go(m):
                got, gave, own = kvl.at[self.l, iminus(m), 1 - k], kvl.at[self.l, iminus(m), k], kvl.at[self.l, i, k]
                rc(got, got, self.b + m - 1, sib).wait_recv()
                rc(gave, gave, self.b + m - 1, sib).wait_send()
                rc(own, own, self.a + m - 1, chip(m)).wait_send()
            each(go)

    class KeyGrads:
        def __init__(self, l):
            self.l = l
            self.s = move(dkv.at[:, 1 - k], dkr0.at[l], dkr0.at[l], sib)
            self.a = sems(7)

        def out(self, m):
            return rc(dkv.at[iplus(m), k], dkr1.at[self.l, m - 1], self.a + m - 1, chip(m))

        def one(self):
            starts(self.s)

        def two(self):
            recvs(self.s)

            def go(m):
                j = iplus(m)
                for h in range(KV_HEADS):
                    total = dkv[j, k, h].astype(f32) + dkr0[self.l, j, h].astype(f32)
                    dkv[j, k, h] = total.astype(bf16)
                self.out(m).start()

            each(go)

        def three(self):
            each(lambda m: self.out(m).wait())
            sents(self.s)

        def total(self, h):
            val = dkv[i, k, h].astype(f32) + dkr0[self.l, i, h].astype(f32)
            for m in range(7):
                val = val + dkr1[self.l, m, h].astype(f32)
            return val

    class Grads:
        def __init__(self, l, early):
            self.l, self.early = l, early
            self.base, self.n = (0, 16) if early else (16, 8)
            there = rs0.at[l, pl.ds(self.base, self.n)]
            self.s = move(land.at[l, 1 - k, pl.ds(self.base, self.n)], there, there, sib)
            self.r1, self.r2, self.fin = (r1e, r2e, fine) if early else (r1l, r2l, finl)
            self.a, self.b, self.c, self.v, self.z = sems(7), sems(7), sems(7), sems(7), sems(1)
            own = self.fin.at[l, i, k]
            self.t = move(own, own, self.fin.at[l, i, 1 - k], sib)

        def out1(self, m):
            l = self.l
            if self.early:
                q, o = lax.rem(m - 1, 2), (m - 1) // 2
                x_ = near(x, o + 1)
                src, to = land.at[l, k, pl.ds(0, 16), 4 * q + x_], {"dp": zl * 4 + x_}
                return rc(src, r1e.at[l, q, o], self.a + m - 1, to)
            return rc(land.at[l, k, 16 + iplus(m)], r1l.at[l, m - 1], self.a + m - 1, chip(m))

        def outz(self):
            src = land.at[self.l, k, pl.ds(0, 16), 4 * (1 - zl) + x]
            return rc(src, rz.at[self.l], self.z, {"dp": 4 * (1 - zl) + x})

        def out2(self, m):
            l = self.l
            if self.early:
                src, to = land.at[l, k, pl.ds(2 * iplus(m), 2), d], chip(m)
            else:
                src, to = land.at[l, k, 16 + i, dplus(m)], shard(m)
            return rc(src, self.r2.at[l, m - 1], self.b + m - 1, to)

        def zero(self):
            starts(self.s)

        def one(self):
            recvs(self.s)
            l = self.l

            def go(u):
                total = land[l, k, self.base + u].astype(f32) + rs0[l, self.base + u].astype(f32)
                land[l, k, self.base + u] = total.astype(bf16)

            each(go, 0, self.n)

        def send(self):
            each(lambda m: self.out1(m).start(), 1, 7 if self.early else 8)

        def two(self):
            each(lambda m: self.out1(m).wait(), 1, 7 if self.early else 8)
            l = self.l
            if self.early:
                def go(u):
                    for q in range(2):
                        total = land[l, k, u, 4 * q + x].astype(f32)
                        for o in range(3):
                            total = total + r1e[l, q, o, u].astype(f32)
                        land[l, k, u, 4 * q + x] = total.astype(bf16)

                each(go, 0, 16)
                self.outz().start()
            else:
                def go(u):
                    total = land[l, k, 16 + i, u].astype(f32)
                    for m in range(7):
                        total = total + r1l[l, m, u].astype(f32)
                    land[l, k, 16 + i, u] = total.astype(bf16)

                each(go, 0, 8)
                each(lambda m: self.out2(m).start())

        def pair(self):
            self.outz().wait()
            l = self.l

            def go(u):
                land[l, k, u, d] = (land[l, k, u, d].astype(f32) + rz[l, u].astype(f32)).astype(bf16)

            each(go, 0, 16)
            each(lambda m: self.out2(m).start())

        def three(self):
            each(lambda m: self.out2(m).wait())
            l = self.l
            for u in range(2 if self.early else 1):
                total = (land[l, k, 2 * i + u, d] if self.early else land[l, k, 16 + i, d]).astype(f32)
                for m in range(7):
                    total = total + (self.r2[l, m, u] if self.early else self.r2[l, m]).astype(f32)
                self.fin[l, i, k, u] = total.astype(bf16)
            own = self.fin.at[l, i, k]
            each(lambda m: rc(own, own, self.c + m - 1, chip(m)).start())
            starts(self.t)

        def four(self):
            def go(m):
                ref = self.fin.at[self.l, iminus(m), k]
                rc(ref, ref, self.c + m - 1, chip(m)).wait_recv()
                rc(ref, ref, self.v + m - 1, sib).start()
            each(go)

        def five(self):
            l = self.l
            recvs(self.t)
            sents(self.t, self.s)

            def go(m):
                got, gave = self.fin.at[l, iminus(m), 1 - k], self.fin.at[l, iminus(m), k]
                own = self.fin.at[l, i, k]
                rc(got, got, self.v + m - 1, sib).wait_recv()
                rc(gave, gave, self.v + m - 1, sib).wait_send()
                rc(own, own, self.c + m - 1, chip(m)).wait_send()
            each(go)
            for cc in range(NC):
                i_, k_ = cc // 2, cc % 2
                for q, j in enumerate((2 * i_, 2 * i_ + 1) if self.early else (16 + i_,)):
                    val = self.fin[l, i_, k_, q].astype(f32)
                    kind, t = j // 6, 6 * k_ + j % 6
                    cols = slice(128 * t, 128 * t + 128)
                    if kind == 0:
                        ggate[l, :, cols] = val[0:72]
                    elif kind == 1:
                        gup[l, :, cols] = val[0:72]
                    elif kind == 2:
                        at = slice(16 * t, 16 * t + 16)
                        for lt in range(4):
                            gdown[l, at, 128 * lt:128 * lt + 128] = val[16 * lt:16 * lt + 16]
                        gdown[l, at, 512:576] = val[64:80, 0:64]
                    else:
                        gattn[l, :, cols] = val[0:72]
                        if t == 0:
                            ggains[l] = val[72:80]

    weights = {
        (0, "A"): Weights(0, None, (18, 6)), (0, "F"): Weights(0, (0, 3), (12, 6)),
        (1, "A"): Weights(1, (18, 1), (22, 2)), (1, "F"): Weights(1, (0, 3), (12, 6)),
    }
    keys = [Keys(l) for l in range(LAYERS)]
    key_grads = [KeyGrads(l) for l in range(LAYERS)]
    grads = {(l, e): Grads(l, e) for l in range(LAYERS) for e in (True, False)}

    barrier = pltpu.get_barrier_semaphore()

    def hello(m):
        pl.semaphore_signal(barrier, inc=1, device_id=shard(m), device_id_type=MESH)
        pl.semaphore_signal(barrier, inc=1, device_id=chip(m), device_id_type=MESH)

    each(hello)
    pl.semaphore_signal(barrier, inc=1, device_id=sib, device_id_type=MESH)
    pack_attn(0)
    pl.semaphore_wait(barrier, 15)
    weights[0, "A"].one(0)
    pack_ffn(0)
    weights[0, "F"].one(0)
    pack_attn(1)
    pack_ffn(1)

    lane = lax.broadcasted_iota(jnp.int32, (128, 128), 1)
    low_half = lane < 64
    first_quarter = lax.rem(lane, 64) < 32
    cos_q = cosm[...]
    sin_q = sinm[...]
    cos_kv = jnp.where(low_half, cos_q, 1.0)
    sin_kv = jnp.where(low_half, sin_q, 0.0)

    def swap(x):
        return jnp.where(first_quarter, pltpu.roll(x, 96, axis=1), pltpu.roll(x, 32, axis=1))

    row = lax.broadcasted_iota(jnp.int32, (1024, 192), 0) - 64 * c
    col = lax.rem(lax.broadcasted_iota(jnp.int32, (1024, 192), 1), 64)
    bias[...] = jnp.where((row > col) & (row < 64), NEG, 0.0).astype(bf16)
    mk[...] = jnp.concatenate([mlow[...], mlow[:, 0:64]], axis=1).astype(f32)
    row = lax.broadcasted_iota(jnp.int32, (64, 192), 0)
    col = lax.rem(lax.broadcasted_iota(jnp.int32, (64, 192), 1), 64)
    tri = jnp.where(row > col, NEG, 0.0)
    zpad[...] = jnp.zeros((128, PD), bf16)

    def unit(l, u):
        return land[l, lax.rem(u, 12) // 6, 6 * (u // 12) + lax.rem(u, 6)].reshape(PD, 128)

    def pair(l, u):
        return jnp.concatenate([unit(l, u), unit(l, u + 1)], axis=1)

    def units(l, u, n):
        return jnp.concatenate([unit(l, u + j) for j in range(n)], axis=1)

    def norm_scale(h):
        return lax.rsqrt(jnp.mean(h * h, axis=-1, keepdims=True) + eps_norm)

    def spread(x):
        return nn(x.astype(bf16), e1[...]).astype(bf16)

    def unspread(x):
        hi = x.astype(bf16)
        lo = (x - hi.astype(f32)).astype(bf16)
        return nt(hi, e1[...]) + nt(lo, e1[...])

    def set_unit(l, u, val):
        land[l, lax.rem(u, 12) // 6, 6 * (u // 12) + lax.rem(u, 6)] = val.reshape(8, R, 128)

    def load_gains(l):
        total = jnp.zeros((8, PD), f32)
        for s in range(ND):
            part = land[l, 0, 18, s].astype(f32)[72:80, :]
            wide = jnp.concatenate([part, jnp.zeros((8, PD - 128), f32)], axis=1)
            total = total + (pltpu.roll(wide, 72 * s, axis=1) if s else wide)
        gain[l] = total

    def regroup_down(l):
        def go(j):
            src = lax.rem(j, 12)
            for lt in range(5):
                wd[j // 16, pl.ds(pl.multiple_of(lax.rem(j, 16) * 16, 16), 16), 128 * lt:128 * lt + 128] = land[
                    l, src // 6, 12 + lax.rem(src, 6), j // 12, 16 * lt:16 * lt + 16, :
                ]
        each(go, 0, 96)

    def scatter_down(l):
        def go(j):
            src = lax.rem(j, 12)
            for lt in range(5):
                land[l, src // 6, 12 + lax.rem(src, 6), j // 12, 16 * lt:16 * lt + 16, :] = wd[
                    j // 16, pl.ds(pl.multiple_of(lax.rem(j, 16) * 16, 16), 16), 128 * lt:128 * lt + 128
                ]
        each(go, 0, 96)

    def tiles(l, h, j):
        tlo = kvl[l, pl.ds(2 * j, 2), :, h, 0].reshape(256, 128)
        thi = kvl[l, pl.ds(2 * j, 2), :, h, 1].reshape(256, 128)
        m = mlow[pl.ds(pl.multiple_of(256 * j, 256), 256), :]
        x2 = jnp.concatenate([tlo * m, thi * (1 - m)], axis=1)
        return tlo, x2, m

    def swiglu_parts(l, t, x):
        g = nn(x, pair(l, 2 * t))
        u = nn(x, pair(l, 12 + 2 * t))
        return g, u

    def forward(l, h):
        hs[l] = h
        if l == 0:
            weights[0, "A"].two()
        weights[l, "A"].five()
        load_gains(l)
        apad[l] = spread(h * norm_scale(h) * gain[l, 0:1, 0:D])
        a = apad[l]
        for s in range(KV_HEADS):
            kv = nn(a, unit(l, 45 + s))
            kv = kv * cos_kv + swap(kv) * sin_kv
            kvl[l, i, k, s] = kv.astype(bf16).reshape(2, 64, 128)
        keys[l].one()
        if l == 0:
            weights[0, "F"].one(1)
        else:
            weights[1, "F"].two()
        for t in range(5):
            q = nn(a, unit(l, 40 + t))
            q = (q * cos_q + swap(q) * sin_q) * HEAD_DIM ** (-0.5)
            for j in ((2 * t - 1, 2 * t) if t else (0,)):
                part = q if j % 2 else pltpu.roll(q, 64, axis=1)
                part = jnp.where(low_half, part, 0.0).astype(bf16)
                g = j % 3
                qc[l, j // 3, 64 * g:64 * g + 64, 0:128] = part[0:64]
                qc[l, j // 3, 64 * g:64 * g + 64, 128:256] = part[64:128]
        keys[l].two()
        if l == 0:
            for name in ("A", "F"):
                weights[1, name].one(0)
                weights[1, name].one(1)
        keys[l].three()

        def head(s):
            qcat = qc[l, s]
            qT = qcat.astype(f32).T.astype(bf16)
            qhT = qT[128:256]
            top_own = kvl[l, i, k, s, 1]
            se = nn(top_own, qhT) + tri

            def scores(j, carry):
                ml, mh = carry
                tlo, x2, _ = tiles(l, s, j)
                at = pl.ds(pl.multiple_of(256 * j, 256), 256)
                a1 = nn(tlo, qhT)
                a2 = nn(x2, qT) + bias[at, :].astype(f32)
                s1[at, 0:192] = a1
                s2[at, 0:192] = a2
                is_low = mk[at, :] > 0.5
                ml = jnp.maximum(ml, jnp.max(jnp.where(is_low, a2, NEG), axis=0, keepdims=True))
                mh = jnp.maximum(
                    mh, jnp.max(jnp.maximum(a1, jnp.where(is_low, NEG, a2)), axis=0, keepdims=True)
                )
                return ml, mh

            ml, mh = lax.fori_loop(
                0, 4, scores,
                (jnp.full((1, 192), NEG, f32), jnp.max(se, axis=0, keepdims=True)),
            )
            pe = jnp.exp(se - mh)
            acc1[...] = tn(top_own, pe.astype(bf16))
            acc2[...] = jnp.zeros((256, 192), f32)

            def weigh(j, carry):
                ll, lh = carry
                tlo, x2, _ = tiles(l, s, j)
                at = pl.ds(pl.multiple_of(256 * j, 256), 256)
                is_low = mk[at, :] > 0.5
                p1 = jnp.exp(s1[at, 0:192] - mh)
                p2 = jnp.exp(s2[at, 0:192] - jnp.where(is_low, ml, mh))
                ll = ll + jnp.sum(jnp.where(is_low, p2, 0.0), axis=0, keepdims=True)
                lh = lh + jnp.sum(p1 + jnp.where(is_low, 0.0, p2), axis=0, keepdims=True)
                acc1[...] += tn(tlo, p1.astype(bf16))
                acc2[...] += tn(x2, p2.astype(bf16))
                return ll, lh

            ll, lh = lax.fori_loop(
                0, 4, weigh, (jnp.zeros((1, 192), f32), jnp.sum(pe, axis=0, keepdims=True))
            )
            olow = acc2[64:128, :] / ll
            ohigh = (acc2[192:256, :] + acc1[64:128, :]) / lh
            oT[l, s, 0:64, :] = olow
            oT[l, s, 64:128, :] = ohigh
            lse[l, s, 0:1, :] = ml + jnp.log(ll)
            lse[l, s, 1:2, :] = mh + jnp.log(lh)
            zero = jnp.zeros((64, 192), f32)
            tl = jnp.concatenate([zero, olow], axis=0).T.astype(bf16)
            th = jnp.concatenate([zero, ohigh], axis=0).T.astype(bf16)
            for g in range(3):
                oz[3 * s + g, 0:64, :] = tl[64 * g:64 * g + 64]
                oz[3 * s + g, 64:128, :] = th[64 * g:64 * g + 64]

            if l == 0:
                @pl.when(s == 0)
                def _():
                    weights[0, "F"].two()

                @pl.when(s == 1)
                def _():
                    weights[0, "F"].three()
            else:
                @pl.when(s == 1)
                def _():
                    weights[1, "F"].three()

        each(head, 0, KV_HEADS)
        mixp[l] = nt(jnp.concatenate([oz[j] for j in range(HEADS)], axis=1), e2[...]).astype(bf16)
        out = nn(mixp[l], units(l, 36, 5))
        h1 = h + out[:, 0:D]
        h1s[l] = h1
        bpad[l] = spread(h1 * norm_scale(h1) * gain[l, 1:2, 0:D])
        weights[l, "F"].four()
        weights[l, "F"].five()
        if l == 0:
            weights[1, "A"].two()
        regroup_down(l)

        def ffn(t, total):
            g, u = swiglu_parts(l, t, bpad[l])
            if l == LAYERS - 1:
                s1[pl.ds(pl.multiple_of(128 * t, 128), 128), :] = g
                s2[pl.ds(pl.multiple_of(128 * t, 128), 128), :] = u
            m = (g / (1.0 + jnp.exp(-g)) * u).astype(bf16)
            mid[l, t] = m
            if l == 0:
                @pl.when(t == 3)
                def _():
                    weights[1, "A"].three()

            return total + nn(m, wd[t])

        total = lax.fori_loop(0, 6, ffn, jnp.zeros((128, PD), f32))
        if l == 0:
            weights[1, "A"].four()
        return h1 + total[:, 0:D]

    def norm_back(h, g, dn, gain_row):
        r = norm_scale(h)
        xn = h * r
        cc = dn * gain_row
        return (
            g + r * (cc - xn * jnp.mean(cc * xn, axis=-1, keepdims=True)),
            jnp.sum(dn * xn, axis=0, keepdims=True),
        )

    def backward(l, g):
        zpad[:, 0:D] = g.astype(bf16)
        if l < LAYERS - 1:
            regroup_down(l)
        bT = bpad[l].T

        def ffn(t, total):
            dz = zpad[...]
            if l == LAYERS - 1:
                at = pl.ds(pl.multiple_of(128 * t, 128), 128)
                ga, u = s1[at, :], s2[at, :]
            else:
                ga, u = swiglu_parts(l, t, bpad[l])
            dm = nt(dz, wd[t])
            sg = 1.0 / (1.0 + jnp.exp(-ga))
            silu = ga * sg
            dg = (dm * u * (sg * (1.0 + ga * (1.0 - sg)))).astype(bf16)
            du = (dm * silu).astype(bf16)
            total = total + nt(dg, pair(l, 2 * t)) + nt(du, pair(l, 12 + 2 * t))
            wd[t] = tn(mid[l, t], dz).astype(bf16)
            gw = nn(bT, dg).astype(bf16)
            set_unit(l, 2 * t, gw[:, 0:128])
            set_unit(l, 2 * t + 1, gw[:, 128:256])
            gw = nn(bT, du).astype(bf16)
            set_unit(l, 12 + 2 * t, gw[:, 0:128])
            set_unit(l, 13 + 2 * t, gw[:, 128:256])
            return total

        total = lax.fori_loop(0, 6, ffn, jnp.zeros((128, PD), f32))
        scatter_down(l)
        grads[l, True].zero()
        if l < LAYERS - 1:
            grads[l + 1, True].two()
            grads[l + 1, False].one()
            grads[l + 1, False].send()
        dh1, dgain_ffn = norm_back(h1s[l], g, unspread(total), gain[l, 1:2, 0:D])
        zpad[:, 0:D] = dh1.astype(bf16)
        do = nt(zpad[...], units(l, 36, 5)).astype(bf16)
        go = nn(mixp[l].T, zpad[...]).astype(bf16)
        for t in range(4):
            set_unit(l, 36 + t, go[:, 128 * t:128 * t + 128])
        go4[...] = go[:, 512:640]
        for j in range(HEADS):
            part = nn(do, e2[:, 128 * j:128 * j + 128]).astype(bf16)
            gidx = j % 3
            doc[j // 3, 64 * gidx:64 * gidx + 64, 0:128] = part[0:64]
            doc[j // 3, 64 * gidx:64 * gidx + 64, 128:256] = part[64:128]

        def head(s):
            qcat = qc[l, s]
            qh = qcat[:, 128:256]
            qT = qcat.astype(f32).T.astype(bf16)
            qhT = qT[128:256]
            docat = doc[s]
            doh = docat[:, 128:256]
            doT = docat.astype(f32).T
            doTb = doT.astype(bf16)
            dohT = doTb[128:256]
            dl = jnp.sum(oT[l, s, 0:64, :] * doT[64:128, :], axis=0, keepdims=True)
            dh = jnp.sum(oT[l, s, 64:128, :] * doT[192:256, :], axis=0, keepdims=True)
            lsl = lse[l, s, 0:1, :]
            lsh = lse[l, s, 1:2, :]
            own = kvl[l, i, k, s, 1]
            pe = jnp.exp(nn(own, qhT) + tri - lsh)
            dse = (pe * (nn(own, dohT) - dh)).astype(bf16)
            dxe = nn(dse, qh) + nn(pe.astype(bf16), doh)
            acc1[...] = tn(own, dse)
            acc2[...] = jnp.zeros((256, 192), f32)

            def chunk(j):
                tlo, x2, m = tiles(l, s, j)
                at = pl.ds(pl.multiple_of(256 * j, 256), 256)
                is_low = mk[at, :] > 0.5
                p1 = jnp.exp(nn(tlo, qhT) - lsh)
                p2 = jnp.exp(nn(x2, qT) + bias[at, :].astype(f32) - jnp.where(is_low, lsl, lsh))
                ds1 = (p1 * (nn(tlo, dohT) - dh)).astype(bf16)
                ds2 = (p2 * (nn(x2, doTb) - jnp.where(is_low, dl, dh))).astype(bf16)
                p1 = p1.astype(bf16)
                p2 = p2.astype(bf16)
                dx1 = nn(ds1, qh) + nn(p1, doh)
                dx2 = nn(ds2, qcat) + nn(p2, docat)
                mf = m.astype(f32)
                lo = dx1 + mf * dx2[:, 0:128]
                hi = (1.0 - mf) * dx2[:, 128:256]
                dkv[pl.ds(2 * j, 2), :, s, 0] = lo.astype(bf16).reshape(2, 2, 64, 128)
                dkv[pl.ds(2 * j, 2), :, s, 1] = hi.astype(bf16).reshape(2, 2, 64, 128)
                acc1[...] += tn(tlo, ds1)
                acc2[...] += tn(x2, ds2)

            each(chunk, 0, 4)
            dkv[i, k, s, 1] = dxe.astype(bf16)
            zero = jnp.zeros((64, 192), f32)
            tl = jnp.concatenate([acc2[0:64, :], zero], axis=0).T
            th = jnp.concatenate([acc2[128:192, :] + acc1[0:64, :], zero], axis=0).T
            scale = HEAD_DIM ** (-0.5)
            for gidx in range(3):
                dqz[3 * s + gidx, 0:64, :] = tl[64 * gidx:64 * gidx + 64] * scale
                dqz[3 * s + gidx, 64:128, :] = th[64 * gidx:64 * gidx + 64] * scale

            @pl.when(s == 1)
            def _():
                grads[l, True].one()
                if l < LAYERS - 1:
                    grads[l + 1, True].pair()

        each(head, 0, KV_HEADS)
        kg = key_grads[l]
        kg.one()
        kg.two()
        grads[l, True].send()

        rot = []
        for j in range(HEADS):
            t = dqz[j]
            rot.append(t * cos_q - swap(t) * sin_q)
        dq = [pltpu.roll(rot[0], 64, axis=1).astype(bf16)]
        for t in range(1, 5):
            dq.append((rot[2 * t - 1] + pltpu.roll(rot[2 * t], 64, axis=1)).astype(bf16))
        dq = jnp.concatenate(dq, axis=1)
        aT = apad[l].T
        gq = nn(aT, dq).astype(bf16)
        if l < LAYERS - 1:
            grads[l + 1, True].three()
        kg.three()
        dkv_in = []
        for s in range(KV_HEADS):
            t = kg.total(s).reshape(128, 128)
            dkv_in.append((t * cos_kv - swap(t) * sin_kv).astype(bf16))
        dkv_in = jnp.concatenate(dkv_in, axis=1)
        da = nt(dq, units(l, 40, 5)) + nt(dkv_in, units(l, 45, 3))
        set_unit(l, 40, gq[:, 0:128] + go4[...])
        for t in range(1, 5):
            set_unit(l, 40 + t, gq[:, 128 * t:128 * t + 128])
        gkv = nn(aT, dkv_in).astype(bf16)
        for t in range(3):
            set_unit(l, 45 + t, gkv[:, 128 * t:128 * t + 128])
        dh, dgain_attn = norm_back(hs[l], dh1, unspread(da), gain[l, 0:1, 0:D])
        rows = jnp.concatenate([dgain_attn, dgain_ffn, jnp.zeros((6, D), f32)], axis=0)
        rows = jnp.concatenate([rows, jnp.zeros((8, PD - D), f32)], axis=1)
        for s in range(ND):
            part = (pltpu.roll(rows, PD - 72 * s, axis=1) if s else rows)[:, 0:128]
            keep = land[l, 0, 18, s].astype(f32)[0:72, :]
            land[l, 0, 18, s] = jnp.concatenate([keep, part], axis=0).astype(bf16)
        grads[l, False].zero()
        return dh

    h = hid[...].astype(f32)
    h = forward(0, h)
    h = forward(1, h)
    hout[...] = h.astype(bf16)
    g = backward(1, gout[...].astype(f32))
    g = backward(0, g)
    ghid[...] = g
    grads[1, False].two()
    grads[0, False].one()
    grads[0, False].send()
    grads[1, True].four()
    grads[0, True].two()
    grads[1, True].five()
    grads[1, False].three()
    grads[0, True].pair()
    grads[1, False].four()
    grads[0, False].two()
    grads[0, True].three()
    grads[1, False].five()
    grads[0, False].three()
    grads[0, True].four()
    grads[0, True].five()
    grads[0, False].four()
    grads[0, False].five()


def body(
    hidden_in, positions, attn_gain, w_query, w_key, w_value, w_output, ffn_gain, w_gate, w_up, w_down, grad_out
):
    own = lax.dynamic_slice_in_dim(positions, lax.axis_index("ctx") * ROWS, ROWS)
    half = HEAD_DIM // 2
    freq = jnp.exp(-jnp.log(rope_base) * (2.0 * jnp.arange(half, dtype=f32) / HEAD_DIM))
    angle = own.astype(f32)[:, None] * jnp.tile(freq, 4)[None, :]
    sign = jnp.tile(jnp.where(jnp.arange(HEAD_DIM) < half, -1.0, 1.0), 2).astype(f32)
    cosm, sinm = jnp.cos(angle), jnp.sin(angle) * sign[None, :]
    low = (positions.reshape(NC, ROWS)[:, 0] <= own[0]).astype(bf16)
    mlow = jnp.broadcast_to(low[:, None, None], (NC, 64, 128)).reshape(NC * 64, 128)
    spread = np.zeros((D, PD), np.float32)
    for s in range(ND):
        spread[72 * s + np.arange(72), R * s + np.arange(72)] = 1
    heads = np.zeros((PD, 128 * HEADS), np.float32)
    for t in range(D):
        heads[R * (t // 72) + t % 72, 128 * (t // 64) + 64 + t % 64] = 1
    gains = jnp.stack([attn_gain, ffn_gain], axis=1).astype(f32)
    gains = jnp.pad(gains, ((0, 0), (0, 6), (0, 56)))
    kv = jnp.stack(
        [w_key.reshape(LAYERS, 72, KV_HEADS, HEAD_DIM), w_value.reshape(LAYERS, 72, KV_HEADS, HEAD_DIM)], axis=3
    ).reshape(LAYERS, 72, 2 * KV_HEADS * HEAD_DIM)
    wattn = jnp.concatenate([w_output, w_query, kv], axis=2)
    outs = pl.pallas_call(
        kernel,
        out_shape=(
            jax.ShapeDtypeStruct((ROWS, D), bf16),
            jax.ShapeDtypeStruct((ROWS, D), f32),
            jax.ShapeDtypeStruct((LAYERS, 8, 128), f32),
            jax.ShapeDtypeStruct((LAYERS, 72, FF), f32),
            jax.ShapeDtypeStruct((LAYERS, 72, FF), f32),
            jax.ShapeDtypeStruct((LAYERS, 192, D), f32),
            jax.ShapeDtypeStruct((LAYERS, 72, FF), f32),
        ),
        in_specs=[pl.BlockSpec(memory_space=pltpu.VMEM)] * 12,
        out_specs=tuple([pl.BlockSpec(memory_space=pltpu.VMEM)] * 7),
        scratch_shapes=[
            pltpu.VMEM((LAYERS, 2, 24, ND, R, 128), bf16),
            pltpu.VMEM((6, 256, PD), bf16),
            pltpu.VMEM((LAYERS, NCHIP, 2, KV_HEADS, 2, 64, 128), bf16),
            pltpu.VMEM((NCHIP, 2, KV_HEADS, 2, 64, 128), bf16),
            pltpu.VMEM((LAYERS, NCHIP, KV_HEADS, 2, 64, 128), bf16),
            pltpu.VMEM((LAYERS, 7, KV_HEADS, 2, 64, 128), bf16),
            pltpu.VMEM((LAYERS, 24, ND, R, 128), bf16),
            pltpu.VMEM((LAYERS, 2, 3, 16, R, 128), bf16),
            pltpu.VMEM((LAYERS, 16, R, 128), bf16),
            pltpu.VMEM((LAYERS, 7, 2, R, 128), bf16),
            pltpu.VMEM((LAYERS, 7, ND, R, 128), bf16),
            pltpu.VMEM((LAYERS, 7, R, 128), bf16),
            pltpu.VMEM((LAYERS, NCHIP, 2, 2, R, 128), bf16),
            pltpu.VMEM((LAYERS, NCHIP, 2, 1, R, 128), bf16),
            pltpu.VMEM((LAYERS, 6, 128, 256), bf16),
            pltpu.VMEM((LAYERS, 128, D), f32),
            pltpu.VMEM((LAYERS, 128, D), f32),
            pltpu.VMEM((LAYERS, 128, PD), bf16),
            pltpu.VMEM((LAYERS, 128, PD), bf16),
            pltpu.VMEM((LAYERS, 128, PD), bf16),
            pltpu.VMEM((LAYERS, KV_HEADS, 192, 256), bf16),
            pltpu.VMEM((KV_HEADS, 192, 256), bf16),
            pltpu.VMEM((LAYERS, KV_HEADS, 128, 192), f32),
            pltpu.VMEM((LAYERS, KV_HEADS, 8, 192), f32),
            pltpu.VMEM((HEADS, 128, 128), bf16),
            pltpu.VMEM((HEADS, 128, 128), f32),
            pltpu.VMEM((1024, 256), f32),
            pltpu.VMEM((1024, 256), f32),
            pltpu.VMEM((1024, 192), bf16),
            pltpu.VMEM((1024, 192), f32),
            pltpu.VMEM((128, PD), bf16),
            pltpu.VMEM((LAYERS, 8, PD), f32),
            pltpu.VMEM((128, 192), f32),
            pltpu.VMEM((256, 192), f32),
            pltpu.VMEM((PD, 128), bf16),
            pltpu.SemaphoreType.DMA((288,)),
            pltpu.SemaphoreType.DMA((288,)),
        ],
        compiler_params=pltpu.CompilerParams(
            collective_id=0, has_side_effects=True, vmem_limit_bytes=63 * 1024 * 1024
        ),
    )(
        hidden_in, grad_out, cosm, sinm, mlow, jnp.asarray(spread, bf16), jnp.asarray(heads, bf16), gains,
        w_gate, w_up, w_down, wattn,
    )
    hout, ghid, ggains, ggate, gup, gdown, gattn = outs
    gkv = gattn[:, :, 2 * D:].reshape(LAYERS, 72, KV_HEADS, 2, HEAD_DIM)
    return (
        hout,
        ghid,
        ggains[:, 0, 0:72],
        gattn[:, :, D:2 * D],
        gkv[:, :, :, 0].reshape(LAYERS, 72, KV_HEADS * HEAD_DIM),
        gkv[:, :, :, 1].reshape(LAYERS, 72, KV_HEADS * HEAD_DIM),
        gattn[:, :, 0:D],
        ggains[:, 1, 0:72],
        ggate,
        gup,
        gdown,
    )


def solution(mesh):
    placed = (
        P(("dp", "ctx"), None),
        P("dp"),
        P(None, "dp"),
        P(None, "dp", None),
        P(None, "dp", None),
        P(None, "dp", None),
        P(None, "dp", None),
        P(None, "dp"),
        P(None, "dp", None),
        P(None, "dp", None),
        P(None, "dp", None),
        P(("dp", "ctx"), None),
    )
    out = (
        P(("dp", "ctx"), None),
        P(("dp", "ctx"), None),
        P(None, "dp"),
        P(None, "dp", None),
        P(None, "dp", None),
        P(None, "dp", None),
        P(None, "dp", None),
        P(None, "dp"),
        P(None, "dp", None),
        P(None, "dp", None),
        P(None, "dp", None),
    )
    return jax.shard_map(body, mesh=mesh, in_specs=placed, out_specs=out, check_vma=False)
```

time: 381 us -> 293 us (0.77)
  Pallas kernels: 355 us -> 269 us
    pallas_call x1, Pallas kernels: 355 us -> 269 us  [body(): pl.pallas_call(kernel, out_shape=(jax.ShapeDtypeStruct((ROWS, D), bf16),...]
where the time goes in v2:
time: 293 us; the launch traced here: 292 us
  Pallas kernels  269 us (92%)
  local copies, waits for them, and re-layouts  19.7 us (7%)
  other arithmetic  3.4 us (1%)
    pallas_call x1, Pallas kernels, body(): pl.pallas_call(kernel, out_shape=(jax.ShapeDtypeStruct((ROWS, D), bf16),...  269 us
    unnamed x27, local copies, waits for them, and re-layouts  10.6 us

profile of v2, /device:TPU:1, one launch (start us, length us, event | category | flops | bytes accessed | tf_op | source)
XLA Modules:
  0.0 292.5 jit_solution(4864366513018071242)
XLA Ops:
  0.8 0.9 fusion.10
  1.7 0.8 fusion.9
  2.6 0.7 copy.44
  3.2 0.7 copy.45
  4.1 0.6 fusion.8.gains
  4.7 1.0 copy.46
  5.7 1.0 copy.47
  7.2 1.0 fusion
  8.1 0.8 copy.49.hid
  9.0 0.8 copy.50.gout
  9.8 0.9 broadcast_in_dim.23.mlow
  10.7 0.9 concatenate.3.wattn
  11.6 268.6 %shard_map.221 = (bf16[128,576]{1,0:T(8,128)(2,1)}, f32[128,576]{1,0:T(8,128)}, f32[2,8,128]{2,1,0:T(8,128)}, f32[2,72,1536]{2,1,0:T(8,128)}, f32[2,72,1536]{2,1...) custom-call(bf16[128,576]{1,0:T(8,128)(2,1)} %copy.49.hid, bf16[128,576]{1,0:T(8,128)(2,1)} %copy.50.gout, ...), custom_call_target="tpu_custom_call" | custom-call | tf_op jit(solution)/shard_map/pallas_call | solution.py:873
  280.3 1.7 copy.53
  281.9 1.3 fusion.13
  283.3 1.0 slice.31
  284.2 2.1 fusion.11
  286.6 0.3 fusion.12
  287.1 0.8 copy.56
  288.0 0.8 copy.55
  288.8 0.9 copy.54
  289.7 0.9 copy.60
  290.6 0.9 copy.61
  291.5 0.9 copy.62
  (30 shorter events, 1.3 us)
Async XLA Ops:
  0.6 8.3 %copy-start.7 = (bf16[128,576]{0,1:T(8,128)(2,1)S(1)}, bf16[128,576]{0,1:T(8,128)(2,1)}, u32[]{:S(2)}) copy-start(bf16[128,576]{0,1:T(8,128)(2,1)} %param.25) | copy-start | bytes 442372
  0.7 10.0 %copy-start.4 = (bf16[2,72,576]{2,1,0:T(8,128)(2,1)S(1)}, bf16[2,72,576]{2,1,0:T(8,128)(2,1)}, u32[]{:S(2)}) copy-start(bf16[2,72,576]{2,1,0:T(8,128)(2,1)} %param.20) | copy-start | bytes 497668
  0.7 10.0 %copy-start.5 = (bf16[2,72,576]{2,1,0:T(8,128)(2,1)S(1)}, bf16[2,72,576]{2,1,0:T(8,128)(2,1)}, u32[]{:S(2)}) copy-start(bf16[2,72,576]{2,1,0:T(8,128)(2,1)} %param.17) | copy-start | bytes 497668
  0.7 7.5 %copy-start.6 = (bf16[128,576]{0,1:T(8,128)(2,1)S(1)}, bf16[128,576]{0,1:T(8,128)(2,1)}, u32[]{:S(2)}) copy-start(bf16[128,576]{0,1:T(8,128)(2,1)} %param.14) | copy-start | bytes 442372
  286.3 2.5 copy-start.3
  286.6 3.1 %copy-start.2 = (f32[2,72,1536]{2,1,0:T(8,128)S(1)}, f32[2,72,1536]{2,1,0:T(8,128)}, u32[]{:S(2)}) copy-start(f32[2,72,1536]{2,1,0:T(8,128)} %get-tuple-element.87) | copy-start | bytes 2654212
  287.9 2.7 copy-start.1
  289.7 1.8 copy-start

commit v3 on v2

--- a/solution.py
+++ b/solution.py
@@ -1,6 +1,5 @@
 import jax
 import jax.numpy as jnp
-import numpy as np
 from jax import lax
 from jax.experimental import pallas as pl
 from jax.experimental.pallas import tpu as pltpu
@@ -53,11 +52,20 @@
         self.out().wait_send()
 
 
+def slot_of(shard):
+    return (shard % 4) * 2 + shard // 4
+
+
+def attn_place(t):
+    return (t // 2, 18 + t % 2) if t < 4 else ((t - 4) // 4, 20 + (t - 4) % 4)
+
+
 def kernel(
-    hid, gout, cosm, sinm, mlow, e1, e2, gains, wgate, wup, wdown, wattn,
-    hout, ghid, ggains, ggate, gup, gdown, gattn,
+    hidT, goutT, pos, freq, again, fgain, wgate, wup, wdown, wo, wq, wk, wv,
+    hout, ghid, oute, outl,
+    mlow, e1, e2, gains, wattn,
     land, wd, kvl, dkv, dkr0, dkr1,
-    rs0, r1e, rz, r2e, r1l, r2l, fine, finl,
+    rs0, r1e, rz, r2e, r1l, rzl, r2l, fine, finl,
     mid, hs, h1s, apad, bpad, mixp, qc, doc, oT, lse, oz, dqz,
     s1, s2, bias, mk, zpad, gain, acc1, acc2, go4,
     send, recv,
@@ -66,6 +74,7 @@
     c = lax.axis_index("ctx")
     k, y = lax.rem(c, 2), lax.rem(c // 2, 4)
     x, zl = lax.rem(d, 4), d // 4
+    mine = 2 * x + zl
     i = c // 2
     sib = {"ctx": i * 2 + 1 - k}
     count = [0]
@@ -84,6 +93,9 @@
 
     def shard(m):
         return {"dp": dplus(m)}
+
+    def slot(j):
+        return lax.rem(j, 4) * 2 + j // 4
 
     def chip(m):
         return {"ctx": iplus(m) * 2 + k}
@@ -127,19 +139,28 @@
 
     def put(l, j, val, last=None, k=k):
         last = jnp.zeros((8, 128), f32) if last is None else last
-        land[l, k, j, d] = jnp.concatenate([val.astype(f32), last], axis=0).astype(bf16)
+        land[l, k, j, mine] = jnp.concatenate([val.astype(f32), last], axis=0).astype(bf16)
 
     def column(t):
         return pl.ds(pl.multiple_of(128 * t, 128), 128)
 
     def pack_attn(l):
+        key, value = wk[l].astype(f32), wv[l].astype(f32)
+        parts = [wo[l].astype(f32), wq[l].astype(f32)]
+        for h in range(KV_HEADS):
+            parts += [key[:, 64 * h:64 * h + 64], value[:, 64 * h:64 * h + 64]]
+        wattn[...] = jnp.concatenate(parts, axis=1).astype(bf16)
+        gains[l] = jnp.zeros((8, 128), f32)
+        gains[l, 0:1, 0:72] = again[l:l + 1, :].astype(f32)
+        gains[l, 1:2, 0:72] = fgain[l:l + 1, :].astype(f32)
         if l == 0:
             for t in range(12):
-                put(l, 18 + t % 6, wattn[l, :, 128 * t:128 * t + 128], gains[l], t // 6)
+                k_, j = attn_place(t)
+                put(l, j, wattn[:, 128 * t:128 * t + 128], gains[l], k_)
         else:
-            put(l, 18 + y, wattn[l, :, column(6 * k + y)], gains[l])
-            put(l, 22, wattn[l, :, column(6 * k + 4)])
-            put(l, 23, wattn[l, :, column(6 * k + 5)])
+            put(l, 18 + y, wattn[:, column(jnp.where(y < 2, 2 * k + y, 2 + 4 * k + y))], gains[l])
+            put(l, 22, wattn[:, column(6 + 4 * k)])
+            put(l, 23, wattn[:, column(7 + 4 * k)])
 
     def pack_ffn(l):
         @pl.when(y < 2)
@@ -156,7 +177,7 @@
             val = wdown[l, pl.ds(pl.multiple_of(16 * (6 * k + g), 16), 16), :]
             val = jnp.concatenate([val.astype(f32), jnp.zeros((16, 64), f32)], axis=1).astype(bf16)
             for lt in range(5):
-                land[l, k, 12 + g, d, 16 * lt:16 * lt + 16, :] = val[:, 128 * lt:128 * lt + 128]
+                land[l, k, 12 + g, mine, 16 * lt:16 * lt + 16, :] = val[:, 128 * lt:128 * lt + 128]
 
     class Weights:
         def __init__(self, l, shared, direct):
@@ -192,18 +213,22 @@
 
         def one(self, part):
             ref, s = self.parts[part]
-            each(lambda m: rc(ref(d), ref(d), s + m - 1, shard(m)).start())
-
-        def two(self):
+            each(lambda m: rc(ref(mine), ref(mine), s + m - 1, shard(m)).start())
+
+        def two(self, part):
+            ref, s = self.parts[part]
+
             def go(m):
-                for ref, s in self.parts:
-                    own = ref(dminus(m))
-                    rc(own, own, s + m - 1, shard(m)).wait_recv()
-                    if not self.shared:
-                        rc(own, own, self.base + m - 1, sib).start()
+                own = ref(slot(dminus(m)))
+                rc(own, own, s + m - 1, shard(m)).wait_recv()
+                if not self.shared:
+                    rc(own, own, self.base + m - 1, sib).start()
+
             each(go)
-            if self.shared:
-                starts(self.u[0], self.u[1], self.v[0], self.v[1])
+            if part:
+                starts(self.u[0], self.u[1], self.v[1])
+            elif self.shared:
+                starts(self.v[0])
 
         def three(self):
             recvs(self.u[0])
@@ -223,9 +248,9 @@
 
             def go(m):
                 for ref, s in self.parts:
-                    rc(ref(d), ref(d), s + m - 1, shard(m)).wait_send()
+                    rc(ref(mine), ref(mine), s + m - 1, shard(m)).wait_send()
                 if not self.shared:
-                    got, gave = self.slot(1 - k, dminus(m)), self.slot(k, dminus(m))
+                    got, gave = self.slot(1 - k, slot(dminus(m))), self.slot(k, slot(dminus(m)))
                     rc(got, got, self.base + m - 1, sib).wait_recv()
                     rc(gave, gave, self.base + m - 1, sib).wait_send()
             each(go)
@@ -296,89 +321,100 @@
     class Grads:
         def __init__(self, l, early):
             self.l, self.early = l, early
-            self.base, self.n = (0, 16) if early else (16, 8)
-            there = rs0.at[l, pl.ds(self.base, self.n)]
-            self.s = move(land.at[l, 1 - k, pl.ds(self.base, self.n)], there, there, sib)
+            self.own = 16 + y + 4 * (i // 4)
+            self.s = []
+            for lo, n in ((0, 16),) if early else ((16, 4), (20, 4)):
+                there = rs0.at[l, pl.ds(lo, n)]
+                self.s.append(move(land.at[l, 1 - k, pl.ds(lo, n)], there, there, sib))
             self.r1, self.r2, self.fin = (r1e, r2e, fine) if early else (r1l, r2l, finl)
-            self.a, self.b, self.c, self.v, self.z = sems(7), sems(7), sems(7), sems(7), sems(1)
+            self.a, self.b, self.c, self.v, self.z = sems(12), sems(7), sems(7), sems(7), sems(1)
             own = self.fin.at[l, i, k]
             self.t = move(own, own, self.fin.at[l, i, 1 - k], sib)
 
         def out1(self, m):
             l = self.l
             if self.early:
-                q, o = lax.rem(m - 1, 2), (m - 1) // 2
+                h, o = (m - 1) // 3, lax.rem(m - 1, 3)
                 x_ = near(x, o + 1)
-                src, to = land.at[l, k, pl.ds(0, 16), 4 * q + x_], {"dp": zl * 4 + x_}
-                return rc(src, r1e.at[l, q, o], self.a + m - 1, to)
-            return rc(land.at[l, k, 16 + iplus(m)], r1l.at[l, m - 1], self.a + m - 1, chip(m))
+                src, to = land.at[l, k, pl.ds(8 * h, 8), pl.ds(2 * x_, 2)], {"dp": zl * 4 + x_}
+                return rc(src, r1e.at[l, o, pl.ds(8 * h, 8)], self.a + m - 1, to)
+            h, o = (m - 1) // 3, lax.rem(m - 1, 3)
+            y_ = near(y, o + 1)
+            to = {"ctx": ((i // 4) * 4 + y_) * 2 + k}
+            return rc(land.at[l, k, 16 + 4 * h + y_], r1l.at[l, o, h], self.a + m - 1, to)
 
         def outz(self):
-            src = land.at[self.l, k, pl.ds(0, 16), 4 * (1 - zl) + x]
+            if not self.early:
+                src = land.at[self.l, k, 16 + y + 4 * (1 - i // 4)]
+                return rc(src, rzl.at[self.l], self.z, {"ctx": ((1 - i // 4) * 4 + y) * 2 + k})
+            src = land.at[self.l, k, pl.ds(0, 16), 2 * x + 1 - zl]
             return rc(src, rz.at[self.l], self.z, {"dp": 4 * (1 - zl) + x})
 
         def out2(self, m):
             l = self.l
             if self.early:
-                src, to = land.at[l, k, pl.ds(2 * iplus(m), 2), d], chip(m)
+                src, to = land.at[l, k, pl.ds(2 * iplus(m), 2), mine], chip(m)
             else:
-                src, to = land.at[l, k, 16 + i, dplus(m)], shard(m)
+                src, to = land.at[l, k, self.own, slot(dplus(m))], shard(m)
             return rc(src, self.r2.at[l, m - 1], self.b + m - 1, to)
 
-        def zero(self):
-            starts(self.s)
-
-        def one(self):
-            recvs(self.s)
+        def zero(self, part=0):
+            starts(self.s[part])
+
+        def one(self, part=0):
+            recvs(self.s[part])
             l = self.l
 
             def go(u):
-                total = land[l, k, self.base + u].astype(f32) + rs0[l, self.base + u].astype(f32)
-                land[l, k, self.base + u] = total.astype(bf16)
-
-            each(go, 0, self.n)
-
-        def send(self):
-            each(lambda m: self.out1(m).start(), 1, 7 if self.early else 8)
+                total = land[l, k, u].astype(f32) + rs0[l, u].astype(f32)
+                land[l, k, u] = total.astype(bf16)
+
+            each(go, *((0, 16) if self.early else (16 + 4 * part, 20 + 4 * part)))
+
+        def send(self, lo=1, hi=None):
+            each(lambda m: self.out1(m).start(), lo, hi or 7)
 
         def two(self):
-            each(lambda m: self.out1(m).wait(), 1, 7 if self.early else 8)
+            each(lambda m: self.out1(m).wait(), 1, 7)
             l = self.l
             if self.early:
                 def go(u):
-                    for q in range(2):
-                        total = land[l, k, u, 4 * q + x].astype(f32)
-                        for o in range(3):
-                            total = total + r1e[l, q, o, u].astype(f32)
-                        land[l, k, u, 4 * q + x] = total.astype(bf16)
+                    total = land[l, k, u, pl.ds(2 * x, 2)].astype(f32)
+                    for o in range(3):
+                        total = total + r1e[l, o, u].astype(f32)
+                    land[l, k, u, pl.ds(2 * x, 2)] = total.astype(bf16)
 
                 each(go, 0, 16)
-                self.outz().start()
             else:
                 def go(u):
-                    total = land[l, k, 16 + i, u].astype(f32)
-                    for m in range(7):
-                        total = total + r1l[l, m, u].astype(f32)
-                    land[l, k, 16 + i, u] = total.astype(bf16)
+                    for q in range(2):
+                        total = land[l, k, 16 + y + 4 * q, u].astype(f32)
+                        for m in range(3):
+                            total = total + r1l[l, m, q, u].astype(f32)
+                        land[l, k, 16 + y + 4 * q, u] = total.astype(bf16)
 
                 each(go, 0, 8)
-                each(lambda m: self.out2(m).start())
+            self.outz().start()
 
         def pair(self):
             self.outz().wait()
             l = self.l
 
             def go(u):
-                land[l, k, u, d] = (land[l, k, u, d].astype(f32) + rz[l, u].astype(f32)).astype(bf16)
-
-            each(go, 0, 16)
+                if self.early:
+                    land[l, k, u, mine] = (land[l, k, u, mine].astype(f32) + rz[l, u].astype(f32)).astype(bf16)
+                else:
+                    total = land[l, k, self.own, u].astype(f32) + rzl[l, u].astype(f32)
+                    land[l, k, self.own, u] = total.astype(bf16)
+
+            each(go, 0, 16 if self.early else 8)
             each(lambda m: self.out2(m).start())
 
         def three(self):
             each(lambda m: self.out2(m).wait())
             l = self.l
             for u in range(2 if self.early else 1):
-                total = (land[l, k, 2 * i + u, d] if self.early else land[l, k, 16 + i, d]).astype(f32)
+                total = (land[l, k, 2 * i + u, mine] if self.early else land[l, k, self.own, mine]).astype(f32)
                 for m in range(7):
                     total = total + (self.r2[l, m, u] if self.early else self.r2[l, m]).astype(f32)
                 self.fin[l, i, k, u] = total.astype(bf16)
@@ -396,7 +432,7 @@
         def five(self):
             l = self.l
             recvs(self.t)
-            sents(self.t, self.s)
+            sents(self.t, *self.s)
 
             def go(m):
                 got, gave = self.fin.at[l, iminus(m), 1 - k], self.fin.at[l, iminus(m), k]
@@ -405,28 +441,9 @@
                 rc(gave, gave, self.v + m - 1, sib).wait_send()
                 rc(own, own, self.c + m - 1, chip(m)).wait_send()
             each(go)
-            for cc in range(NC):
-                i_, k_ = cc // 2, cc % 2
-                for q, j in enumerate((2 * i_, 2 * i_ + 1) if self.early else (16 + i_,)):
-                    val = self.fin[l, i_, k_, q].astype(f32)
-                    kind, t = j // 6, 6 * k_ + j % 6
-                    cols = slice(128 * t, 128 * t + 128)
-                    if kind == 0:
-                        ggate[l, :, cols] = val[0:72]
-                    elif kind == 1:
-                        gup[l, :, cols] = val[0:72]
-                    elif kind == 2:
-                        at = slice(16 * t, 16 * t + 16)
-                        for lt in range(4):
-                            gdown[l, at, 128 * lt:128 * lt + 128] = val[16 * lt:16 * lt + 16]
-                        gdown[l, at, 512:576] = val[64:80, 0:64]
-                    else:
-                        gattn[l, :, cols] = val[0:72]
-                        if t == 0:
-                            ggains[l] = val[72:80]
 
     weights = {
-        (0, "A"): Weights(0, None, (18, 6)), (0, "F"): Weights(0, (0, 3), (12, 6)),
+        (0, "A"): Weights(0, None, (20, 4)), (0, "O"): Weights(0, None, (18, 2)), (0, "F"): Weights(0, (0, 3), (12, 6)),
         (1, "A"): Weights(1, (18, 1), (22, 2)), (1, "F"): Weights(1, (0, 3), (12, 6)),
     }
     keys = [Keys(l) for l in range(LAYERS)]
@@ -445,15 +462,32 @@
     pl.semaphore_wait(barrier, 15)
     weights[0, "A"].one(0)
     pack_ffn(0)
-    weights[0, "F"].one(0)
+    weights[0, "F"].one(1)
     pack_attn(1)
     pack_ffn(1)
 
     lane = lax.broadcasted_iota(jnp.int32, (128, 128), 1)
     low_half = lane < 64
     first_quarter = lax.rem(lane, 64) < 32
-    cos_q = cosm[...]
-    sin_q = sinm[...]
+    place_own = pos[pl.ds(c, 1), :].astype(f32)
+    angle = jnp.broadcast_to(place_own, (128, 128)).T * freq[...]
+    cos_q = jnp.cos(angle)
+    sin_q = jnp.sin(angle) * jnp.where(first_quarter, -1.0, 1.0)
+    low = jnp.where(pos[:, 0:1] <= pos[pl.ds(c, 1), 0:1], 1.0, 0.0)
+    for s in range(NC):
+        mlow[64 * s:64 * s + 64, :] = jnp.broadcast_to(low[s:s + 1, :], (64, 128)).astype(bf16)
+    row = lax.broadcasted_iota(jnp.int32, (D, PD), 0)
+    col = lax.broadcasted_iota(jnp.int32, (D, PD), 1)
+    shard_of = (row * 911) >> 16
+    e1[...] = jnp.where(
+        col == row - 72 * shard_of + R * ((shard_of & 3) * 2 + (shard_of >> 2)), 1.0, 0.0
+    ).astype(bf16)
+    row = lax.broadcasted_iota(jnp.int32, (PD, 128 * HEADS), 0)
+    col = lax.broadcasted_iota(jnp.int32, (PD, 128 * HEADS), 1)
+    at_slot = (row * 205) >> 14
+    natural = row - R * at_slot + 72 * ((at_slot & 1) * 4 + (at_slot >> 1))
+    hit = (row - R * at_slot < 72) & (col == 128 * (natural >> 6) + 64 + (natural & 63))
+    e2[...] = jnp.where(hit, 1.0, 0.0).astype(bf16)
     cos_kv = jnp.where(low_half, cos_q, 1.0)
     sin_kv = jnp.where(low_half, sin_q, 0.0)
 
@@ -469,8 +503,13 @@
     tri = jnp.where(row > col, NEG, 0.0)
     zpad[...] = jnp.zeros((128, PD), bf16)
 
+    def place(u):
+        if isinstance(u, int) and u >= 36:
+            return attn_place(u - 36)
+        return lax.rem(u, 12) // 6, 6 * (u // 12) + lax.rem(u, 6)
+
     def unit(l, u):
-        return land[l, lax.rem(u, 12) // 6, 6 * (u // 12) + lax.rem(u, 6)].reshape(PD, 128)
+        return land[(l, *place(u))].reshape(PD, 128)
 
     def pair(l, u):
         return jnp.concatenate([unit(l, u), unit(l, u + 1)], axis=1)
@@ -490,33 +529,39 @@
         return nt(hi, e1[...]) + nt(lo, e1[...])
 
     def set_unit(l, u, val):
-        land[l, lax.rem(u, 12) // 6, 6 * (u // 12) + lax.rem(u, 6)] = val.reshape(8, R, 128)
+        land[(l, *place(u))] = val.reshape(8, R, 128)
 
     def load_gains(l):
         total = jnp.zeros((8, PD), f32)
         for s in range(ND):
-            part = land[l, 0, 18, s].astype(f32)[72:80, :]
+            part = land[l, 0, 20, slot_of(s)].astype(f32)[72:80, :]
             wide = jnp.concatenate([part, jnp.zeros((8, PD - 128), f32)], axis=1)
             total = total + (pltpu.roll(wide, 72 * s, axis=1) if s else wide)
         gain[l] = total
 
+    def down_pieces(l, f):
+        def go(g):
+            for k_ in range(2):
+                for s in range(ND):
+                    for lt in range(5):
+                        f(
+                            wd.at[12 * s + 6 * k_ + g, :, 128 * lt:128 * lt + 128],
+                            land.at[l, k_, 12 + g, slot_of(s), 16 * lt:16 * lt + 16, :],
+                        )
+        each(go, 0, 6)
+
     def regroup_down(l):
-        def go(j):
-            src = lax.rem(j, 12)
-            for lt in range(5):
-                wd[j // 16, pl.ds(pl.multiple_of(lax.rem(j, 16) * 16, 16), 16), 128 * lt:128 * lt + 128] = land[
-                    l, src // 6, 12 + lax.rem(src, 6), j // 12, 16 * lt:16 * lt + 16, :
-                ]
-        each(go, 0, 96)
+        def go(rows, piece):
+            rows[...] = piece[...]
+        down_pieces(l, go)
 
     def scatter_down(l):
-        def go(j):
-            src = lax.rem(j, 12)
-            for lt in range(5):
-                land[l, src // 6, 12 + lax.rem(src, 6), j // 12, 16 * lt:16 * lt + 16, :] = wd[
-                    j // 16, pl.ds(pl.multiple_of(lax.rem(j, 16) * 16, 16), 16), 128 * lt:128 * lt + 128
-                ]
-        each(go, 0, 96)
+        def go(rows, piece):
+            piece[...] = rows[...]
+        down_pieces(l, go)
+
+    def down(t):
+        return wd[pl.ds(16 * t, 16)].reshape(256, PD)
 
     def tiles(l, h, j):
         tlo = kvl[l, pl.ds(2 * j, 2), :, h, 0].reshape(256, 128)
@@ -533,7 +578,7 @@
     def forward(l, h):
         hs[l] = h
         if l == 0:
-            weights[0, "A"].two()
+            weights[0, "A"].two(0)
         weights[l, "A"].five()
         load_gains(l)
         apad[l] = spread(h * norm_scale(h) * gain[l, 0:1, 0:D])
@@ -543,10 +588,9 @@
             kv = kv * cos_kv + swap(kv) * sin_kv
             kvl[l, i, k, s] = kv.astype(bf16).reshape(2, 64, 128)
         keys[l].one()
-        if l == 0:
-            weights[0, "F"].one(1)
-        else:
-            weights[1, "F"].two()
+        if l == 1:
+            weights[1, "F"].two(1)
+            weights[1, "F"].two(0)
         for t in range(5):
             q = nn(a, unit(l, 40 + t))
             q = (q * cos_q + swap(q) * sin_q) * HEAD_DIM ** (-0.5)
@@ -558,9 +602,9 @@
                 qc[l, j // 3, 64 * g:64 * g + 64, 128:256] = part[64:128]
         keys[l].two()
         if l == 0:
-            for name in ("A", "F"):
-                weights[1, name].one(0)
-                weights[1, name].one(1)
+            weights[0, "F"].two(1)
+            weights[0, "O"].one(0)
+            weights[0, "F"].one(0)
         keys[l].three()
 
         def head(s):
@@ -625,26 +669,35 @@
             if l == 0:
                 @pl.when(s == 0)
                 def _():
-                    weights[0, "F"].two()
+                    weights[1, "A"].one(1)
+                    weights[1, "A"].one(0)
 
                 @pl.when(s == 1)
                 def _():
                     weights[0, "F"].three()
+                    weights[0, "O"].two(0)
+                    weights[1, "F"].one(1)
+                    weights[1, "F"].one(0)
             else:
                 @pl.when(s == 1)
                 def _():
                     weights[1, "F"].three()
 
         each(head, 0, KV_HEADS)
+        if l == 0:
+            weights[0, "F"].two(0)
+            weights[0, "F"].four()
+            weights[0, "O"].five()
         mixp[l] = nt(jnp.concatenate([oz[j] for j in range(HEADS)], axis=1), e2[...]).astype(bf16)
         out = nn(mixp[l], units(l, 36, 5))
         h1 = h + out[:, 0:D]
         h1s[l] = h1
         bpad[l] = spread(h1 * norm_scale(h1) * gain[l, 1:2, 0:D])
-        weights[l, "F"].four()
+        if l == 0:
+            weights[1, "A"].two(1)
+        else:
+            weights[1, "F"].four()
         weights[l, "F"].five()
-        if l == 0:
-            weights[1, "A"].two()
         regroup_down(l)
 
         def ffn(t, total):
@@ -659,10 +712,11 @@
                 def _():
                     weights[1, "A"].three()
 
-            return total + nn(m, wd[t])
+            return total + nn(m, down(t))
 
         total = lax.fori_loop(0, 6, ffn, jnp.zeros((128, PD), f32))
         if l == 0:
+            weights[1, "A"].two(0)
             weights[1, "A"].four()
         return h1 + total[:, 0:D]
 
@@ -688,13 +742,13 @@
                 ga, u = s1[at, :], s2[at, :]
             else:
                 ga, u = swiglu_parts(l, t, bpad[l])
-            dm = nt(dz, wd[t])
+            dm = nt(dz, down(t))
             sg = 1.0 / (1.0 + jnp.exp(-ga))
             silu = ga * sg
             dg = (dm * u * (sg * (1.0 + ga * (1.0 - sg)))).astype(bf16)
             du = (dm * silu).astype(bf16)
             total = total + nt(dg, pair(l, 2 * t)) + nt(du, pair(l, 12 + 2 * t))
-            wd[t] = tn(mid[l, t], dz).astype(bf16)
+            wd[pl.ds(16 * t, 16)] = tn(mid[l, t], dz).astype(bf16).reshape(16, 16, PD)
             gw = nn(bT, dg).astype(bf16)
             set_unit(l, 2 * t, gw[:, 0:128])
             set_unit(l, 2 * t + 1, gw[:, 128:256])
@@ -707,9 +761,8 @@
         scatter_down(l)
         grads[l, True].zero()
         if l < LAYERS - 1:
-            grads[l + 1, True].two()
-            grads[l + 1, False].one()
-            grads[l + 1, False].send()
+            grads[l + 1, False].one(1)
+            grads[l + 1, False].send(4, 7)
         dh1, dgain_ffn = norm_back(h1s[l], g, unspread(total), gain[l, 1:2, 0:D])
         zpad[:, 0:D] = dh1.astype(bf16)
         do = nt(zpad[...], units(l, 36, 5)).astype(bf16)
@@ -717,6 +770,7 @@
         for t in range(4):
             set_unit(l, 36 + t, go[:, 128 * t:128 * t + 128])
         go4[...] = go[:, 512:640]
+        grads[l, False].zero(0)
         for j in range(HEADS):
             part = nn(do, e2[:, 128 * j:128 * j + 128]).astype(bf16)
             gidx = j % 3
@@ -776,15 +830,26 @@
 
             @pl.when(s == 1)
             def _():
-                grads[l, True].one()
+                grads[l, False].one(0)
                 if l < LAYERS - 1:
-                    grads[l + 1, True].pair()
-
+                    grads[l, False].send(1, 4)
+                    grads[l + 1, True].two()
+                else:
+                    grads[l, True].one()
+
+        if l < LAYERS - 1:
+            grads[l, True].one()
+            grads[l, True].send(1, 4)
         each(head, 0, KV_HEADS)
         kg = key_grads[l]
         kg.one()
         kg.two()
-        grads[l, True].send()
+        if l < LAYERS - 1:
+            grads[l, True].send(4, 7)
+            grads[l + 1, False].two()
+        else:
+            grads[l, True].send()
+            grads[l, False].send(1, 4)
 
         rot = []
         for j in range(HEADS):
@@ -796,9 +861,9 @@
         dq = jnp.concatenate(dq, axis=1)
         aT = apad[l].T
         gq = nn(aT, dq).astype(bf16)
+        kg.three()
         if l < LAYERS - 1:
-            grads[l + 1, True].three()
-        kg.three()
+            grads[l + 1, True].pair()
         dkv_in = []
         for s in range(KV_HEADS):
             t = kg.total(s).reshape(128, 128)
@@ -816,85 +881,109 @@
         rows = jnp.concatenate([rows, jnp.zeros((8, PD - D), f32)], axis=1)
         for s in range(ND):
             part = (pltpu.roll(rows, PD - 72 * s, axis=1) if s else rows)[:, 0:128]
-            keep = land[l, 0, 18, s].astype(f32)[0:72, :]
-            land[l, 0, 18, s] = jnp.concatenate([keep, part], axis=0).astype(bf16)
-        grads[l, False].zero()
+            keep = land[l, 0, 20, slot_of(s)].astype(f32)[0:72, :]
+            land[l, 0, 20, slot_of(s)] = jnp.concatenate([keep, part], axis=0).astype(bf16)
+        grads[l, False].zero(1)
         return dh
 
-    h = hid[...].astype(f32)
+    h = hidT[...].astype(f32).T
     h = forward(0, h)
     h = forward(1, h)
     hout[...] = h.astype(bf16)
-    g = backward(1, gout[...].astype(f32))
+    g = backward(1, goutT[...].astype(f32).T)
     g = backward(0, g)
     ghid[...] = g
-    grads[1, False].two()
-    grads[0, False].one()
-    grads[0, False].send()
+    grads[0, False].one(1)
+    grads[0, False].send(4, 7)
+    grads[0, True].two()
+    grads[1, False].pair()
+    grads[1, True].three()
+    grads[0, False].two()
+    grads[0, True].pair()
+    grads[1, False].three()
     grads[1, True].four()
-    grads[0, True].two()
     grads[1, True].five()
-    grads[1, False].three()
-    grads[0, True].pair()
+    grads[0, False].pair()
+    grads[0, True].three()
     grads[1, False].four()
-    grads[0, False].two()
-    grads[0, True].three()
     grads[1, False].five()
     grads[0, False].three()
     grads[0, True].four()
     grads[0, True].five()
+    oute[...] = fine[...]
     grads[0, False].four()
     grads[0, False].five()
+    outl[...] = finl[...]
+
+
+def unpack(h, gh, early, late, houtT, ghidT, gag, gq, gk, gv, go, gfg, ggate, gup, gdown):
+    houtT[...] = h[...].astype(f32).T.astype(bf16)
+    ghidT[...] = gh[...].T
+    for l in range(LAYERS):
+        attn = [None] * 12
+        for cc in range(NC):
+            i_, k_ = cc // 2, cc % 2
+            for j in (2 * i_, 2 * i_ + 1, 16 + i_ % 4 + 4 * (i_ // 4)):
+                val = (early[l, i_, k_, j - 2 * i_] if j < 16 else late[l, i_, k_, 0]).astype(f32)
+                kind, t = j // 6, 6 * k_ + j % 6
+                cols = slice(128 * t, 128 * t + 128)
+                if kind == 0:
+                    ggate[l, :, cols] = val[0:72]
+                elif kind == 1:
+                    gup[l, :, cols] = val[0:72]
+                elif kind == 2:
+                    at = slice(16 * t, 16 * t + 16)
+                    for lt in range(4):
+                        gdown[l, at, 128 * lt:128 * lt + 128] = val[16 * lt:16 * lt + 16]
+                    gdown[l, at, 512:576] = val[64:80, 0:64]
+                else:
+                    t = 2 * k_ + j - 18 if j < 20 else 4 + 4 * k_ + j - 20
+                    attn[t] = val[0:72]
+                    if t == 4:
+                        gag[l:l + 1, :] = val[72:73, 0:72]
+                        gfg[l:l + 1, :] = val[73:74, 0:72]
+        attn = jnp.concatenate(attn, axis=1)
+        go[l] = attn[:, 0:D]
+        gq[l] = attn[:, D:2 * D]
+        kv = [attn[:, 2 * D + 64 * j:2 * D + 64 * j + 64] for j in range(2 * KV_HEADS)]
+        gk[l] = jnp.concatenate(kv[0::2], axis=1)
+        gv[l] = jnp.concatenate(kv[1::2], axis=1)
 
 
 def body(
     hidden_in, positions, attn_gain, w_query, w_key, w_value, w_output, ffn_gain, w_gate, w_up, w_down, grad_out
 ):
-    own = lax.dynamic_slice_in_dim(positions, lax.axis_index("ctx") * ROWS, ROWS)
     half = HEAD_DIM // 2
     freq = jnp.exp(-jnp.log(rope_base) * (2.0 * jnp.arange(half, dtype=f32) / HEAD_DIM))
-    angle = own.astype(f32)[:, None] * jnp.tile(freq, 4)[None, :]
-    sign = jnp.tile(jnp.where(jnp.arange(HEAD_DIM) < half, -1.0, 1.0), 2).astype(f32)
-    cosm, sinm = jnp.cos(angle), jnp.sin(angle) * sign[None, :]
-    low = (positions.reshape(NC, ROWS)[:, 0] <= own[0]).astype(bf16)
-    mlow = jnp.broadcast_to(low[:, None, None], (NC, 64, 128)).reshape(NC * 64, 128)
-    spread = np.zeros((D, PD), np.float32)
-    for s in range(ND):
-        spread[72 * s + np.arange(72), R * s + np.arange(72)] = 1
-    heads = np.zeros((PD, 128 * HEADS), np.float32)
-    for t in range(D):
-        heads[R * (t // 72) + t % 72, 128 * (t // 64) + 64 + t % 64] = 1
-    gains = jnp.stack([attn_gain, ffn_gain], axis=1).astype(f32)
-    gains = jnp.pad(gains, ((0, 0), (0, 6), (0, 56)))
-    kv = jnp.stack(
-        [w_key.reshape(LAYERS, 72, KV_HEADS, HEAD_DIM), w_value.reshape(LAYERS, 72, KV_HEADS, HEAD_DIM)], axis=3
-    ).reshape(LAYERS, 72, 2 * KV_HEADS * HEAD_DIM)
-    wattn = jnp.concatenate([w_output, w_query, kv], axis=2)
+    freq = jnp.tile(freq, 4).reshape(1, 128)
     outs = pl.pallas_call(
         kernel,
         out_shape=(
             jax.ShapeDtypeStruct((ROWS, D), bf16),
             jax.ShapeDtypeStruct((ROWS, D), f32),
-            jax.ShapeDtypeStruct((LAYERS, 8, 128), f32),
-            jax.ShapeDtypeStruct((LAYERS, 72, FF), f32),
-            jax.ShapeDtypeStruct((LAYERS, 72, FF), f32),
-            jax.ShapeDtypeStruct((LAYERS, 192, D), f32),
-            jax.ShapeDtypeStruct((LAYERS, 72, FF), f32),
+            jax.ShapeDtypeStruct((LAYERS, NCHIP, 2, 2, R, 128), bf16),
+            jax.ShapeDtypeStruct((LAYERS, NCHIP, 2, 1, R, 128), bf16),
         ),
-        in_specs=[pl.BlockSpec(memory_space=pltpu.VMEM)] * 12,
-        out_specs=tuple([pl.BlockSpec(memory_space=pltpu.VMEM)] * 7),
+        in_specs=[pl.BlockSpec(memory_space=pltpu.VMEM)] * 13,
+        out_specs=tuple([pl.BlockSpec(memory_space=pltpu.VMEM)] * 4),
         scratch_shapes=[
+            pltpu.VMEM((NC * 64, 128), bf16),
+            pltpu.VMEM((D, PD), bf16),
+            pltpu.VMEM((PD, 128 * HEADS), bf16),
+            pltpu.VMEM((LAYERS, 8, 128), f32),
+            pltpu.VMEM((72, FF), bf16),
             pltpu.VMEM((LAYERS, 2, 24, ND, R, 128), bf16),
-            pltpu.VMEM((6, 256, PD), bf16),
+            pltpu.VMEM((96, 16, PD), bf16),
             pltpu.VMEM((LAYERS, NCHIP, 2, KV_HEADS, 2, 64, 128), bf16),
             pltpu.VMEM((NCHIP, 2, KV_HEADS, 2, 64, 128), bf16),
             pltpu.VMEM((LAYERS, NCHIP, KV_HEADS, 2, 64, 128), bf16),
             pltpu.VMEM((LAYERS, 7, KV_HEADS, 2, 64, 128), bf16),
             pltpu.VMEM((LAYERS, 24, ND, R, 128), bf16),
-            pltpu.VMEM((LAYERS, 2, 3, 16, R, 128), bf16),
+            pltpu.VMEM((LAYERS, 3, 16, 2, R, 128), bf16),
             pltpu.VMEM((LAYERS, 16, R, 128), bf16),
             pltpu.VMEM((LAYERS, 7, 2, R, 128), bf16),
-            pltpu.VMEM((LAYERS, 7, ND, R, 128), bf16),
+            pltpu.VMEM((LAYERS, 3, 2, ND, R, 128), bf16),
+            pltpu.VMEM((LAYERS, ND, R, 128), bf16),
             pltpu.VMEM((LAYERS, 7, R, 128), bf16),
             pltpu.VMEM((LAYERS, NCHIP, 2, 2, R, 128), bf16),
             pltpu.VMEM((LAYERS, NCHIP, 2, 1, R, 128), bf16),
@@ -919,31 +1008,29 @@
             pltpu.VMEM((128, 192), f32),
             pltpu.VMEM((256, 192), f32),
             pltpu.VMEM((PD, 128), bf16),
-            pltpu.SemaphoreType.DMA((288,)),
-            pltpu.SemaphoreType.DMA((288,)),
+            pltpu.SemaphoreType.DMA((320,)),
+            pltpu.SemaphoreType.DMA((320,)),
         ],
         compiler_params=pltpu.CompilerParams(
-            collective_id=0, has_side_effects=True, vmem_limit_bytes=63 * 1024 * 1024
+            collective_id=0, has_side_effects=True, vmem_limit_bytes=127 * 512 * 1024
         ),
     )(
-        hidden_in, grad_out, cosm, sinm, mlow, jnp.asarray(spread, bf16), jnp.asarray(heads, bf16), gains,
-        w_gate, w_up, w_down, wattn,
+        hidden_in.T, grad_out.T, positions.reshape(NC, ROWS), freq, attn_gain, ffn_gain,
+        w_gate, w_up, w_down, w_output, w_query, w_key, w_value,
     )
-    hout, ghid, ggains, ggate, gup, gdown, gattn = outs
-    gkv = gattn[:, :, 2 * D:].reshape(LAYERS, 72, KV_HEADS, 2, HEAD_DIM)
-    return (
-        hout,
-        ghid,
-        ggains[:, 0, 0:72],
-        gattn[:, :, D:2 * D],
-        gkv[:, :, :, 0].reshape(LAYERS, 72, KV_HEADS * HEAD_DIM),
-        gkv[:, :, :, 1].reshape(LAYERS, 72, KV_HEADS * HEAD_DIM),
-        gattn[:, :, 0:D],
-        ggains[:, 1, 0:72],
-        ggate,
-        gup,
-        gdown,
+    shapes = (
+        (D, ROWS), (D, ROWS), (LAYERS, 72), (LAYERS, 72, D), (LAYERS, 72, KV_HEADS * HEAD_DIM),
+        (LAYERS, 72, KV_HEADS * HEAD_DIM), (LAYERS, 72, D), (LAYERS, 72), (LAYERS, 72, FF), (LAYERS, 72, FF),
+        (LAYERS, 192, D),
     )
+    houtT, ghidT, *rest = pl.pallas_call(
+        unpack,
+        out_shape=[jax.ShapeDtypeStruct(shape, f32 if n else bf16) for n, shape in enumerate(shapes)],
+        in_specs=[pl.BlockSpec(memory_space=pltpu.VMEM)] * 4,
+        out_specs=[pl.BlockSpec(memory_space=pltpu.VMEM)] * 11,
+        compiler_params=pltpu.CompilerParams(vmem_limit_bytes=127 * 512 * 1024),
+    )(*outs)
+    return (houtT.T, ghidT.T, *rest)
 
 
 def solution(mesh):

time: 293 us -> 232 us (0.79)
  Pallas kernels: 269 us -> 230 us
  local copies, waits for them, and re-layouts: 19.7 us -> 0.6 us
  other arithmetic: 3.4 us -> 0.01 us
    pallas_call x1, Pallas kernels: 269 us -> 226 us  [body(): pl.pallas_call(kernel, out_shape=(jax.ShapeDtypeStruct((ROWS, D), bf16),...]
    unnamed x27 -> x0, local copies, waits for them, and re-layouts: 10.6 us -> none
    slice x6 -> x0, local copies, waits for them, and re-layouts: 4.96 us -> none  [the longest x1 2.09 us: body(): gattn[:, :, 0:D]]
    pallas_call x0 -> x1, Pallas kernels: none -> 3.89 us  [body(): pl.pallas_call(unpack, out_shape=[jax.ShapeDtypeStruct(shape, f32 if n el...]
where the time goes in v3:
time: 232 us
  Pallas kernels  230 us (99%)
    pallas_call x1, Pallas kernels, body(): pl.pallas_call(kernel, out_shape=(jax.ShapeDtypeStruct((ROWS, D), bf16),...  226 us

profile of v3, /device:TPU:1, one launch (start us, length us, event | category | flops | bytes accessed | tf_op | source)
XLA Modules:
  0.0 231.6 jit_solution(3339984977025672952)
XLA Ops:
  0.7 0.6 reshape_tile.3.freq
  1.3 226.5 %shard_map.203 = (bf16[128,576]{1,0:T(8,128)(2,1)}, f32[128,576]{1,0:T(8,128)}, bf16[2,8,2,2,80,128]{5,4,3,2,1,0:T(8,128)(2,1)}, bf16[2,8,2,1,80,128]{5,4,3,2,1,0:T(8,128)(2,1)}) custom-call(bf16[576,128]{1,0:T(8,128)(2,1)} %bitcast.5, bf16[576,128]{1,0:T(8,128)(2,1)} %bitcast.6, s32[16,128]{1,0:T(8,128)} %bitcast.7, f32[1,128]{1,0:T(1,128)} %reshape_tile.3.freq, ...), custom_call_target="tpu_custom_call" | custom-call | tf_op jit(solution)/shard_map/pallas_call | solution.py:959
  227.7 3.9 %shard_map.204 = (bf16[576,128]{1,0:T(8,128)(2,1)}, f32[576,128]{1,0:T(8,128)}, f32[2,72]{1,0:T(2,128)}, f32[2,72,576]{2,1,0:T(8,128)}, f32[2,72,192]{2,1,0:T(8,...) custom-call(bf16[128,576]{1,0:T(8,128)(2,1)} %get-tuple-element.26.h, ...), custom_call_target="tpu_custom_call" | custom-call | tf_op jit(solution)/shard_map/pallas_call | solution.py:1026
  (2 shorter events, 0.0 us)

commit v4 on v3

--- a/solution.py
+++ b/solution.py
@@ -103,6 +103,9 @@
     def near(at, o):
         return lax.rem(at + o + 4, 4)
 
+    def X(o):
+        return {"dp": zl * 4 + near(x, o)}
+
     def Y(o):
         return {"ctx": ((i // 4) * 4 + near(y, o)) * 2 + k}
 
@@ -182,6 +185,7 @@
     class Weights:
         def __init__(self, l, shared, direct):
             self.shared = shared is not None
+            self.relays = (l, direct[0]) != (0, 20)
             db, nd = direct
 
             def straight(slot):
@@ -211,20 +215,41 @@
             ]
             self.v += [move(block(y_), block(y_), block(y_, 1 - k), sib) for y_ in (y, ym, yp, y2)]
 
+        def sends(self, part):
+            ref, s = self.parts[part]
+            if not self.relays:
+                return [(rc(ref(mine), ref(mine), s + m - 1, shard(m)), slot(dminus(m)), s + m - 1, m - 1) for m in range(1, 8)]
+            other = 2 * x + 1 - zl
+            out = [
+                (rc(ref(mine), ref(mine), s + o - 1, X(o)), 2 * near(x, -o) + zl, s + o - 1, o - 1) for o in (1, 2, 3)
+            ]
+            out.append((rc(ref(mine), ref(mine), s + 3, {"dp": (1 - zl) * 4 + x}), other, s + 3, 3))
+            return out + [
+                (rc(ref(other), ref(other), s + 3 + o, X(o)), 2 * near(x, -o) + 1 - zl, s + 3 + o, 3 + o)
+                for o in (1, 2, 3)
+            ]
+
         def one(self, part):
-            ref, s = self.parts[part]
-            each(lambda m: rc(ref(mine), ref(mine), s + m - 1, shard(m)).start())
+            for copy, *_ in self.sends(part)[:4 if self.relays else 7]:
+                copy.start()
+
+        def got(self, part, item):
+            _, at, s, b = item
+            ref = self.parts[part][0](at)
+            rc(ref, ref, s, sib).wait_recv()
+            if not self.shared:
+                rc(ref, ref, self.base + b, sib).start()
+
+        def relay(self, part):
+            sends = self.sends(part)
+            self.got(part, sends[3])
+            for copy, *_ in sends[4:]:
+                copy.start()
 
         def two(self, part):
-            ref, s = self.parts[part]
-
-            def go(m):
-                own = ref(slot(dminus(m)))
-                rc(own, own, s + m - 1, shard(m)).wait_recv()
-                if not self.shared:
-                    rc(own, own, self.base + m - 1, sib).start()
-
-            each(go)
+            for n, item in enumerate(self.sends(part)):
+                if not (self.relays and n == 3):
+                    self.got(part, item)
             if part:
                 starts(self.u[0], self.u[1], self.v[1])
             elif self.shared:
@@ -246,71 +271,78 @@
                 sents(*self.u)
                 sents(*self.v)
 
-            def go(m):
-                for ref, s in self.parts:
-                    rc(ref(mine), ref(mine), s + m - 1, shard(m)).wait_send()
-                if not self.shared:
-                    got, gave = self.slot(1 - k, slot(dminus(m))), self.slot(k, slot(dminus(m)))
-                    rc(got, got, self.base + m - 1, sib).wait_recv()
-                    rc(gave, gave, self.base + m - 1, sib).wait_send()
-            each(go)
+            for part in range(len(self.parts)):
+                for copy, at, _, b in self.sends(part):
+                    copy.wait_send()
+                    if not self.shared:
+                        got, gave = self.slot(1 - k, at), self.slot(k, at)
+                        rc(got, got, self.base + b, sib).wait_recv()
+                        rc(gave, gave, self.base + b, sib).wait_send()
 
     class Keys:
         def __init__(self, l):
-            self.l, self.a, self.b = l, sems(7), sems(7)
-            own = kvl.at[l, i, k]
-            self.s = move(own, own, kvl.at[l, i, 1 - k], sib)
-
-        def one(self):
-            own = kvl.at[self.l, i, k]
-            each(lambda m: rc(own, own, self.a + m - 1, chip(m)).start())
-            starts(self.s)
-
-        def two(self):
+            self.l, self.a, self.b, self.s = l, sems(21), sems(21), sems(3)
+
+        def own(self, h):
+            ref = kvl.at[self.l, i, k, h]
+            return rc(ref, ref, self.s + h, sib)
+
+        def out(self, h, m):
+            ref = kvl.at[self.l, i, k, h]
+            return rc(ref, ref, self.a + 7 * h + m - 1, chip(m))
+
+        def passed(self, h, m, k_):
+            ref = kvl.at[self.l, iminus(m), k_, h]
+            return rc(ref, ref, self.b + 7 * h + m - 1, sib)
+
+        def one(self, h):
+            each(lambda m: self.out(h, m).start())
+            self.own(h).start()
+
+        def two(self, h):
             def go(m):
-                ref = kvl.at[self.l, iminus(m), k]
-                rc(ref, ref, self.a + m - 1, chip(m)).wait_recv()
-                rc(ref, ref, self.b + m - 1, sib).start()
+                ref = kvl.at[self.l, iminus(m), k, h]
+                rc(ref, ref, self.a + 7 * h + m - 1, chip(m)).wait_recv()
+                self.passed(h, m, k).start()
             each(go)
 
-        def three(self):
-            recvs(self.s)
-            sents(self.s)
+        def three(self, h):
+            ref = kvl.at[self.l, i, 1 - k, h]
+            rc(ref, ref, self.s + h, sib).wait_recv()
+            self.own(h).wait_send()
 
             def go(m):
-                got, gave, own = kvl.at[self.l, iminus(m), 1 - k], kvl.at[self.l, iminus(m), k], kvl.at[self.l, i, k]
-                rc(got, got, self.b + m - 1, sib).wait_recv()
-                rc(gave, gave, self.b + m - 1, sib).wait_send()
-                rc(own, own, self.a + m - 1, chip(m)).wait_send()
+                self.passed(h, m, 1 - k).wait_recv()
+                self.passed(h, m, k).wait_send()
+                self.out(h, m).wait_send()
             each(go)
 
     class KeyGrads:
         def __init__(self, l):
-            self.l = l
-            self.s = move(dkv.at[:, 1 - k], dkr0.at[l], dkr0.at[l], sib)
-            self.a = sems(7)
-
-        def out(self, m):
-            return rc(dkv.at[iplus(m), k], dkr1.at[self.l, m - 1], self.a + m - 1, chip(m))
-
-        def one(self):
-            starts(self.s)
-
-        def two(self):
-            recvs(self.s)
+            self.l, self.s, self.a = l, sems(3), sems(21)
+
+        def pair(self, h):
+            return rc(dkv.at[:, 1 - k, h], dkr0.at[self.l, :, h], self.s + h, sib)
+
+        def out(self, h, m):
+            return rc(dkv.at[iplus(m), k, h], dkr1.at[self.l, m - 1, h], self.a + 7 * h + m - 1, chip(m))
+
+        def one(self, h):
+            self.pair(h).start()
+
+        def two(self, h):
+            self.pair(h).wait()
 
             def go(m):
                 j = iplus(m)
-                for h in range(KV_HEADS):
-                    total = dkv[j, k, h].astype(f32) + dkr0[self.l, j, h].astype(f32)
-                    dkv[j, k, h] = total.astype(bf16)
-                self.out(m).start()
+                total = dkv[j, k, h].astype(f32) + dkr0[self.l, j, h].astype(f32)
+                dkv[j, k, h] = total.astype(bf16)
+                self.out(h, m).start()
 
             each(go)
 
-        def three(self):
-            each(lambda m: self.out(m).wait())
-            sents(self.s)
+        def three(self, h):
+            each(lambda m: self.out(h, m).wait())
 
         def total(self, h):
             val = dkv[i, k, h].astype(f32) + dkr0[self.l, i, h].astype(f32)
@@ -580,6 +612,8 @@
         if l == 0:
             weights[0, "A"].two(0)
         weights[l, "A"].five()
+        if l == 0:
+            weights[0, "F"].relay(1)
         load_gains(l)
         apad[l] = spread(h * norm_scale(h) * gain[l, 0:1, 0:D])
         a = apad[l]
@@ -587,10 +621,12 @@
             kv = nn(a, unit(l, 45 + s))
             kv = kv * cos_kv + swap(kv) * sin_kv
             kvl[l, i, k, s] = kv.astype(bf16).reshape(2, 64, 128)
-        keys[l].one()
-        if l == 1:
+            keys[l].one(s)
+        if l == 0:
+            weights[0, "O"].one(0)
+            weights[0, "F"].one(0)
+        else:
             weights[1, "F"].two(1)
-            weights[1, "F"].two(0)
         for t in range(5):
             q = nn(a, unit(l, 40 + t))
             q = (q * cos_q + swap(q) * sin_q) * HEAD_DIM ** (-0.5)
@@ -600,14 +636,17 @@
                 g = j % 3
                 qc[l, j // 3, 64 * g:64 * g + 64, 0:128] = part[0:64]
                 qc[l, j // 3, 64 * g:64 * g + 64, 128:256] = part[64:128]
-        keys[l].two()
+        keys[l].two(0)
         if l == 0:
             weights[0, "F"].two(1)
-            weights[0, "O"].one(0)
-            weights[0, "F"].one(0)
-        keys[l].three()
 
         def head(s):
+            keys[l].three(s)
+
+            @pl.when(s < KV_HEADS - 1)
+            def _():
+                keys[l].two(s + 1)
+
             qcat = qc[l, s]
             qT = qcat.astype(f32).T.astype(bf16)
             qhT = qT[128:256]
@@ -669,22 +708,27 @@
             if l == 0:
                 @pl.when(s == 0)
                 def _():
+                    weights[0, "O"].relay(0)
+                    weights[0, "F"].relay(0)
                     weights[1, "A"].one(1)
                     weights[1, "A"].one(0)
 
                 @pl.when(s == 1)
                 def _():
-                    weights[0, "F"].three()
-                    weights[0, "O"].two(0)
+                    weights[1, "A"].relay(1)
+                    weights[1, "A"].relay(0)
                     weights[1, "F"].one(1)
                     weights[1, "F"].one(0)
             else:
                 @pl.when(s == 1)
                 def _():
+                    weights[1, "F"].two(0)
                     weights[1, "F"].three()
 
         each(head, 0, KV_HEADS)
         if l == 0:
+            weights[0, "F"].three()
+            weights[0, "O"].two(0)
             weights[0, "F"].two(0)
             weights[0, "F"].four()
             weights[0, "O"].five()
@@ -695,6 +739,8 @@
         bpad[l] = spread(h1 * norm_scale(h1) * gain[l, 1:2, 0:D])
         if l == 0:
             weights[1, "A"].two(1)
+            weights[1, "F"].relay(1)
+            weights[1, "F"].relay(0)
         else:
             weights[1, "F"].four()
         weights[l, "F"].five()
@@ -828,28 +874,30 @@
                 dqz[3 * s + gidx, 0:64, :] = tl[64 * gidx:64 * gidx + 64] * scale
                 dqz[3 * s + gidx, 64:128, :] = th[64 * gidx:64 * gidx + 64] * scale
 
+            kg.one(s)
+
+            @pl.when(s == 0)
+            def _():
+                grads[l, True].one()
+                grads[l, True].send()
+                if l < LAYERS - 1:
+                    grads[l + 1, True].two()
+
             @pl.when(s == 1)
             def _():
+                kg.two(0)
                 grads[l, False].one(0)
-                if l < LAYERS - 1:
-                    grads[l, False].send(1, 4)
-                    grads[l + 1, True].two()
-                else:
-                    grads[l, True].one()
-
+
+            @pl.when(s == 2)
+            def _():
+                kg.two(1)
+
+        kg = key_grads[l]
+        each(head, 0, KV_HEADS)
+        kg.two(2)
+        grads[l, False].send(1, 4)
         if l < LAYERS - 1:
-            grads[l, True].one()
-            grads[l, True].send(1, 4)
-        each(head, 0, KV_HEADS)
-        kg = key_grads[l]
-        kg.one()
-        kg.two()
-        if l < LAYERS - 1:
-            grads[l, True].send(4, 7)
             grads[l + 1, False].two()
-        else:
-            grads[l, True].send()
-            grads[l, False].send(1, 4)
 
         rot = []
         for j in range(HEADS):
@@ -861,7 +909,8 @@
         dq = jnp.concatenate(dq, axis=1)
         aT = apad[l].T
         gq = nn(aT, dq).astype(bf16)
-        kg.three()
+        for s in range(KV_HEADS):
+            kg.three(s)
         if l < LAYERS - 1:
             grads[l + 1, True].pair()
         dkv_in = []
@@ -895,24 +944,24 @@
     ghid[...] = g
     grads[0, False].one(1)
     grads[0, False].send(4, 7)
-    grads[0, True].two()
     grads[1, False].pair()
     grads[1, True].three()
+    grads[0, True].two()
     grads[0, False].two()
-    grads[0, True].pair()
     grads[1, False].three()
     grads[1, True].four()
+    grads[0, True].pair()
+    grads[0, False].pair()
     grads[1, True].five()
-    grads[0, False].pair()
+    grads[1, False].four()
     grads[0, True].three()
-    grads[1, False].four()
+    grads[0, False].three()
     grads[1, False].five()
-    grads[0, False].three()
     grads[0, True].four()
+    grads[0, False].four()
     grads[0, True].five()
+    grads[0, False].five()
     oute[...] = fine[...]
-    grads[0, False].four()
-    grads[0, False].five()
     outl[...] = finl[...]
 
 
@@ -1008,8 +1057,8 @@
             pltpu.VMEM((128, 192), f32),
             pltpu.VMEM((256, 192), f32),
             pltpu.VMEM((PD, 128), bf16),
-            pltpu.SemaphoreType.DMA((320,)),
-            pltpu.SemaphoreType.DMA((320,)),
+            pltpu.SemaphoreType.DMA((416,)),
+            pltpu.SemaphoreType.DMA((416,)),
         ],
         compiler_params=pltpu.CompilerParams(
             collective_id=0, has_side_effects=True, vmem_limit_bytes=127 * 512 * 1024

time: 232 us -> 218 us (0.940)
  Pallas kernels: 230 us -> 216 us
    pallas_call x1, Pallas kernels: 226 us -> 212 us  [body(): pl.pallas_call(kernel, out_shape=(jax.ShapeDtypeStruct((ROWS, D), bf16),...]
where the time goes in v4:
time: 218 us; the launch traced here: 217 us
  Pallas kernels  216 us (99%)
    pallas_call x1, Pallas kernels, body(): pl.pallas_call(kernel, out_shape=(jax.ShapeDtypeStruct((ROWS, D), bf16),...  212 us

profile of v4, /device:TPU:1, one launch (start us, length us, event | category | flops | bytes accessed | tf_op | source)
XLA Modules:
  0.0 217.3 jit_solution(1290009301552235374)
XLA Ops:
  0.7 0.6 reshape_tile.3.freq
  1.3 212.2 %shard_map.203 = (bf16[128,576]{1,0:T(8,128)(2,1)}, f32[128,576]{1,0:T(8,128)}, bf16[2,8,2,2,80,128]{5,4,3,2,1,0:T(8,128)(2,1)}, bf16[2,8,2,1,80,128]{5,4,3,2,1,0:T(8,128)(2,1)}) custom-call(bf16[576,128]{1,0:T(8,128)(2,1)} %bitcast.5, bf16[576,128]{1,0:T(8,128)(2,1)} %bitcast.6, s32[16,128]{1,0:T(8,128)} %bitcast.7, f32[1,128]{1,0:T(1,128)} %reshape_tile.3.freq, ...), custom_call_target="tpu_custom_call" | custom-call | tf_op jit(solution)/shard_map/pallas_call | solution.py:1008
  213.4 3.9 %shard_map.204 = (bf16[576,128]{1,0:T(8,128)(2,1)}, f32[576,128]{1,0:T(8,128)}, f32[2,72]{1,0:T(2,128)}, f32[2,72,576]{2,1,0:T(8,128)}, f32[2,72,192]{2,1,0:T(8,...) custom-call(bf16[128,576]{1,0:T(8,128)(2,1)} %get-tuple-element.26.h, ...), custom_call_target="tpu_custom_call" | custom-call | tf_op jit(solution)/shard_map/pallas_call | solution.py:1075
  (2 shorter events, 0.0 us)

commit v5 on v4

--- a/solution.py
+++ b/solution.py
@@ -68,7 +68,7 @@
     rs0, r1e, rz, r2e, r1l, rzl, r2l, fine, finl,
     mid, hs, h1s, apad, bpad, mixp, qc, doc, oT, lse, oz, dqz,
     s1, s2, bias, mk, zpad, gain, acc1, acc2, go4,
-    send, recv,
+    hv, gv, send, recv, leave,
 ):
     d = lax.axis_index("dp")
     c = lax.axis_index("ctx")
@@ -166,16 +166,18 @@
             put(l, 23, wattn[:, column(7 + 4 * k)])
 
     def pack_ffn(l):
-        @pl.when(y < 2)
+        @pl.when(y < 3)
         def _():
-            for r in range(3):
-                put(l, 3 * y + r, wgate[l, :, column(6 * k + 3 * y + r)])
-
-        @pl.when(y >= 2)
+            for r in range(2):
+                put(l, 2 * y + r, wgate[l, :, column(6 * k + 2 * y + r)])
+
+        @pl.when(y == 3)
         def _():
-            for r in range(3):
-                put(l, 3 * y + r, wup[l, :, column(6 * k + 3 * (y - 2) + r)])
-
+            for r in range(2):
+                put(l, 6 + r, wup[l, :, column(6 * k + r)])
+
+        for r in range(2, 6):
+            put(l, 6 + r, wup[l, :, column(6 * k + r)])
         for g in range(6):
             val = wdown[l, pl.ds(pl.multiple_of(16 * (6 * k + g), 16), 16), :]
             val = jnp.concatenate([val.astype(f32), jnp.zeros((16, 64), f32)], axis=1).astype(bf16)
@@ -230,7 +232,8 @@
             ]
 
         def one(self, part):
-            for copy, *_ in self.sends(part)[:4 if self.relays else 7]:
+            sends = self.sends(part)
+            for copy, *_ in [sends[3], *sends[:3]] if self.relays else sends:
                 copy.start()
 
         def got(self, part, item):
@@ -475,8 +478,8 @@
             each(go)
 
     weights = {
-        (0, "A"): Weights(0, None, (20, 4)), (0, "O"): Weights(0, None, (18, 2)), (0, "F"): Weights(0, (0, 3), (12, 6)),
-        (1, "A"): Weights(1, (18, 1), (22, 2)), (1, "F"): Weights(1, (0, 3), (12, 6)),
+        (0, "A"): Weights(0, None, (20, 4)), (0, "O"): Weights(0, None, (18, 2)), (0, "F"): Weights(0, (0, 2), (8, 10)),
+        (1, "A"): Weights(1, (18, 1), (22, 2)), (1, "F"): Weights(1, (0, 2), (8, 10)),
     }
     keys = [Keys(l) for l in range(LAYERS)]
     key_grads = [KeyGrads(l) for l in range(LAYERS)]
@@ -938,10 +941,16 @@
     h = hidT[...].astype(f32).T
     h = forward(0, h)
     h = forward(1, h)
-    hout[...] = h.astype(bf16)
+    hv[...] = h.astype(bf16)
+    outputs = [
+        pltpu.make_async_copy(src, dst, leave.at[n])
+        for n, (src, dst) in enumerate(((hv, hout), (gv, ghid), (fine, oute), (finl, outl)))
+    ]
+    outputs[0].start()
     g = backward(1, goutT[...].astype(f32).T)
     g = backward(0, g)
-    ghid[...] = g
+    gv[...] = g
+    outputs[1].start()
     grads[0, False].one(1)
     grads[0, False].send(4, 7)
     grads[1, False].pair()
@@ -960,9 +969,11 @@
     grads[0, True].four()
     grads[0, False].four()
     grads[0, True].five()
+    outputs[2].start()
     grads[0, False].five()
-    oute[...] = fine[...]
-    outl[...] = finl[...]
+    outputs[3].start()
+    for copy in outputs:
+        copy.wait()
 
 
 def unpack(h, gh, early, late, houtT, ghidT, gag, gq, gk, gv, go, gfg, ggate, gup, gdown):
@@ -1014,7 +1025,7 @@
             jax.ShapeDtypeStruct((LAYERS, NCHIP, 2, 1, R, 128), bf16),
         ),
         in_specs=[pl.BlockSpec(memory_space=pltpu.VMEM)] * 13,
-        out_specs=tuple([pl.BlockSpec(memory_space=pltpu.VMEM)] * 4),
+        out_specs=tuple([pl.BlockSpec(memory_space=pl.ANY)] * 4),
         scratch_shapes=[
             pltpu.VMEM((NC * 64, 128), bf16),
             pltpu.VMEM((D, PD), bf16),
@@ -1057,8 +1068,11 @@
             pltpu.VMEM((128, 192), f32),
             pltpu.VMEM((256, 192), f32),
             pltpu.VMEM((PD, 128), bf16),
-            pltpu.SemaphoreType.DMA((416,)),
-            pltpu.SemaphoreType.DMA((416,)),
+            pltpu.VMEM((ROWS, D), bf16),
+            pltpu.VMEM((ROWS, D), f32),
+            pltpu.SemaphoreType.DMA((381,)),
+            pltpu.SemaphoreType.DMA((381,)),
+            pltpu.SemaphoreType.DMA((4,)),
         ],
         compiler_params=pltpu.CompilerParams(
             collective_id=0, has_side_effects=True, vmem_limit_bytes=127 * 512 * 1024

time: 218 us -> 210 us (0.963)
  Pallas kernels: 216 us -> 209 us
    pallas_call x1, Pallas kernels: 212 us -> 205 us  [body(): pl.pallas_call(kernel, out_shape=(jax.ShapeDtypeStruct((ROWS, D), bf16),...]
where the time goes in v5:
time: 210 us
  Pallas kernels  209 us (100%)
    pallas_call x1, Pallas kernels, body(): pl.pallas_call(kernel, out_shape=(jax.ShapeDtypeStruct((ROWS, D), bf16),...  205 us

profile of v5, /device:TPU:1, one launch (start us, length us, event | category | flops | bytes accessed | tf_op | source)
XLA Modules:
  0.0 210.2 jit_solution(18396547027996926303)
XLA Ops:
  0.7 0.6 reshape_tile.3.freq
  1.3 205.0 %shard_map.203 = (bf16[128,576]{1,0:T(8,128)(2,1)}, f32[128,576]{1,0:T(8,128)}, bf16[2,8,2,2,80,128]{5,4,3,2,1,0:T(8,128)(2,1)}, bf16[2,8,2,1,80,128]{5,4,3,2,1,0:T(8,128)(2,1)}) custom-call(bf16[576,128]{1,0:T(8,128)(2,1)} %bitcast.5, bf16[576,128]{1,0:T(8,128)(2,1)} %bitcast.6, s32[16,128]{1,0:T(8,128)} %bitcast.7, f32[1,128]{1,0:T(1,128)} %reshape_tile.3.freq, ...), custom_call_target="tpu_custom_call" | custom-call | tf_op jit(solution)/shard_map/pallas_call | solution.py:1019
  206.3 3.9 %shard_map.204 = (bf16[576,128]{1,0:T(8,128)(2,1)}, f32[576,128]{1,0:T(8,128)}, f32[2,72]{1,0:T(2,128)}, f32[2,72,576]{2,1,0:T(8,128)}, f32[2,72,192]{2,1,0:T(8,...) custom-call(bf16[128,576]{1,0:T(8,128)(2,1)} %get-tuple-element.26.h, ...), custom_call_target="tpu_custom_call" | custom-call | tf_op jit(solution)/shard_map/pallas_call | solution.py:1089
  (2 shorter events, 0.0 us)

commit v6 on v5

--- a/solution.py
+++ b/solution.py
@@ -362,7 +362,7 @@
                 there = rs0.at[l, pl.ds(lo, n)]
                 self.s.append(move(land.at[l, 1 - k, pl.ds(lo, n)], there, there, sib))
             self.r1, self.r2, self.fin = (r1e, r2e, fine) if early else (r1l, r2l, finl)
-            self.a, self.b, self.c, self.v, self.z = sems(12), sems(7), sems(7), sems(7), sems(1)
+            self.a, self.b, self.c, self.v, self.z = sems(6), sems(7), sems(7), sems(7), sems(2 if early else 1)
             own = self.fin.at[l, i, k]
             self.t = move(own, own, self.fin.at[l, i, 1 - k], sib)
 
@@ -378,12 +378,12 @@
             to = {"ctx": ((i // 4) * 4 + y_) * 2 + k}
             return rc(land.at[l, k, 16 + 4 * h + y_], r1l.at[l, o, h], self.a + m - 1, to)
 
-        def outz(self):
+        def outz(self, h=0):
             if not self.early:
                 src = land.at[self.l, k, 16 + y + 4 * (1 - i // 4)]
                 return rc(src, rzl.at[self.l], self.z, {"ctx": ((1 - i // 4) * 4 + y) * 2 + k})
-            src = land.at[self.l, k, pl.ds(0, 16), 2 * x + 1 - zl]
-            return rc(src, rz.at[self.l], self.z, {"dp": 4 * (1 - zl) + x})
+            src = land.at[self.l, k, pl.ds(8 * h, 8), 2 * x + 1 - zl]
+            return rc(src, rz.at[self.l, pl.ds(8 * h, 8)], self.z + h, {"dp": 4 * (1 - zl) + x})
 
         def out2(self, m):
             l = self.l
@@ -409,8 +409,7 @@
         def send(self, lo=1, hi=None):
             each(lambda m: self.out1(m).start(), lo, hi or 7)
 
-        def two(self):
-            each(lambda m: self.out1(m).wait(), 1, 7)
+        def two(self, halves=(0, 1)):
             l = self.l
             if self.early:
                 def go(u):
@@ -419,8 +418,13 @@
                         total = total + r1e[l, o, u].astype(f32)
                     land[l, k, u, pl.ds(2 * x, 2)] = total.astype(bf16)
 
-                each(go, 0, 16)
+                for h in halves:
+                    each(lambda m: self.out1(m).wait(), 1 + 3 * h, 4 + 3 * h)
+                    each(go, 8 * h, 8 * h + 8)
+                    self.outz(h).start()
             else:
+                each(lambda m: self.out1(m).wait(), 1, 7)
+
                 def go(u):
                     for q in range(2):
                         total = land[l, k, 16 + y + 4 * q, u].astype(f32)
@@ -429,10 +433,11 @@
                         land[l, k, 16 + y + 4 * q, u] = total.astype(bf16)
 
                 each(go, 0, 8)
-            self.outz().start()
+                self.outz().start()
 
         def pair(self):
-            self.outz().wait()
+            for h in range(2 if self.early else 1):
+                self.outz(h).wait()
             l = self.l
 
             def go(u):
@@ -882,9 +887,11 @@
             @pl.when(s == 0)
             def _():
                 grads[l, True].one()
-                grads[l, True].send()
+                grads[l, True].send(1, 4)
                 if l < LAYERS - 1:
                     grads[l + 1, True].two()
+                else:
+                    grads[l, True].send(4, 7)
 
             @pl.when(s == 1)
             def _():
@@ -894,6 +901,8 @@
             @pl.when(s == 2)
             def _():
                 kg.two(1)
+                if l < LAYERS - 1:
+                    grads[l, True].send(4, 7)
 
         kg = key_grads[l]
         each(head, 0, KV_HEADS)
@@ -915,6 +924,7 @@
         for s in range(KV_HEADS):
             kg.three(s)
         if l < LAYERS - 1:
+            grads[l, True].two((0,))
             grads[l + 1, True].pair()
         dkv_in = []
         for s in range(KV_HEADS):
@@ -955,7 +965,7 @@
     grads[0, False].send(4, 7)
     grads[1, False].pair()
     grads[1, True].three()
-    grads[0, True].two()
+    grads[0, True].two((1,))
     grads[0, False].two()
     grads[1, False].three()
     grads[1, True].four()
@@ -1070,8 +1080,8 @@
             pltpu.VMEM((PD, 128), bf16),
             pltpu.VMEM((ROWS, D), bf16),
             pltpu.VMEM((ROWS, D), f32),
-            pltpu.SemaphoreType.DMA((381,)),
-            pltpu.SemaphoreType.DMA((381,)),
+            pltpu.SemaphoreType.DMA((359,)),
+            pltpu.SemaphoreType.DMA((359,)),
             pltpu.SemaphoreType.DMA((4,)),
         ],
         compiler_params=pltpu.CompilerParams(

time: 210 us -> 206 us (0.981)
  Pallas kernels: 209 us -> 204 us
    pallas_call x1, Pallas kernels: 205 us -> 200 us  [body(): pl.pallas_call(kernel, out_shape=(jax.ShapeDtypeStruct((ROWS, D), bf16),...]
where the time goes in v6:
time: 206 us
  Pallas kernels  204 us (99%)
    pallas_call x1, Pallas kernels, body(): pl.pallas_call(kernel, out_shape=(jax.ShapeDtypeStruct((ROWS, D), bf16),...  200 us

profile of v6, /device:TPU:1, one launch (start us, length us, event | category | flops | bytes accessed | tf_op | source)
XLA Modules:
  0.0 205.5 jit_solution(8867293395575044805)
XLA Ops:
  0.7 0.6 reshape_tile.3.freq
  1.3 200.4 %shard_map.203 = (bf16[128,576]{1,0:T(8,128)(2,1)}, f32[128,576]{1,0:T(8,128)}, bf16[2,8,2,2,80,128]{5,4,3,2,1,0:T(8,128)(2,1)}, bf16[2,8,2,1,80,128]{5,4,3,2,1,0:T(8,128)(2,1)}) custom-call(bf16[576,128]{1,0:T(8,128)(2,1)} %bitcast.5, bf16[576,128]{1,0:T(8,128)(2,1)} %bitcast.6, s32[16,128]{1,0:T(8,128)} %bitcast.7, f32[1,128]{1,0:T(1,128)} %reshape_tile.3.freq, ...), custom_call_target="tpu_custom_call" | custom-call | tf_op jit(solution)/shard_map/pallas_call | solution.py:1029
  201.6 3.9 %shard_map.204 = (bf16[576,128]{1,0:T(8,128)(2,1)}, f32[576,128]{1,0:T(8,128)}, f32[2,72]{1,0:T(2,128)}, f32[2,72,576]{2,1,0:T(8,128)}, f32[2,72,192]{2,1,0:T(8,...) custom-call(bf16[128,576]{1,0:T(8,128)(2,1)} %get-tuple-element.26.h, ...), custom_call_target="tpu_custom_call" | custom-call | tf_op jit(solution)/shard_map/pallas_call | solution.py:1099
  (2 shorter events, 0.0 us)
